TPU v7x, 32 devices: a whole 2x2x4 slice. The times are simulated.
32 devices in a mesh: rep: 4 (over y, x), fsdp: 8 (over z, core).
Axes of the slice: x: 2, y: 2, z: 4, core: 2. Of those that a mesh axis runs over, the one named last changes fastest.
Arguments:
- block_input: bfloat16 [4, 2048, 2048], P('rep', 'fsdp')
- cotangent: bfloat16 [4, 2048, 2048], P('rep', 'fsdp'), may hold values from -6 to 6
- glob_select: int32 [4, 64, 2048], P('rep', None, 'fsdp'), may hold values from 0 to 1, as said below
- assignment: int32 [8, 464], P('fsdp'), may hold values from 0 to 463, as said below
- master: float32 [8, 464, 128, 128], P('fsdp', 'rep')
- first_moment: float32 [8, 464, 128, 128], P('fsdp', 'rep')
- second_moment: float32 [8, 464, 128, 128], P('fsdp', 'rep')
- left_basis: float32 [8, 464, 128, 128], P('fsdp', 'rep'), may hold values from -0.5 to 0.5
- right_basis: float32 [8, 464, 128, 128], P('fsdp', 'rep'), may hold values from -0.5 to 0.5
- gains: float32 [2, 2048], replicated, may hold values from 0.5 to 1.5
- gain_first: float32 [2, 2048], replicated, may hold values from -448 to 448
- gain_second: float32 [2, 2048], replicated, may hold values from 5242.88 to 20971.52
Outputs:
- block_output: float32 [4, 2048, 2048], P('rep', 'fsdp')
- input_grad: float32 [4, 2048, 2048], P('rep', 'fsdp')
- new_first_moment: float32 [8, 464, 128, 128], P('fsdp', 'rep')
- new_second_moment: float32 [8, 464, 128, 128], P('fsdp', 'rep')
- new_master: float32 [8, 464, 128, 128], P('fsdp', 'rep')
- master_copy: bfloat16 [8, 464, 128, 128], P('fsdp', 'rep')
- new_gain_first: float32 [2, 2048], replicated
- new_gain_second: float32 [2, 2048], replicated
- new_gains: float32 [2, 2048], replicated
- rms_stats: float32 [3], replicated
Inputs may be any that keep to these rules, and one draw needn't show every extreme that they name: `glob_select`: each of the 64 rows of a sequence holds a single 1, and the rows mark 64 different positions. `assignment`: each row names every slot of its band once.
All inputs are finite; a program needn't handle non-finite values.
Results may differ from a plain program's by a relative error of at most 0.025.
Values may be sent and summed in bfloat16 or wider, within the bound.
A program may use at most 512 MiB of HBM per device.

v0:
```python
import functools

import jax
import jax.numpy as jnp
import numpy as np
from jax import lax
from jax.experimental import pallas as pl
from jax.experimental.layout import Layout, with_layout_constraint
from jax.experimental.pallas import tpu as pltpu
from jax.sharding import PartitionSpec as P

D = 2048
H = 32
KVH = 8
HD = 64
FF = 8192
WINDOW = 512
BLK = 128
STEP = 10


norm_eps = 1e-05
rope_theta = 500000.0
beta_one = 0.5
beta_two = 0.5
adam_eps = 1e-08
weight_decay = 0.1
gain_rate = 0.5
masked_value = -1e30


def matrix_shapes():
    kv_width = KVH * HD
    return [(D, D), (D, kv_width), (D, kv_width), (D, D), (D, FF), (D, FF), (FF, D)]


def kind_rates(band_total):
    rate_list = [
        D ** (-0.5),
        D ** (-0.5),
        D ** (-0.5),
        (D * 8 // WINDOW) ** (-0.5),
        D ** (-0.5),
        D ** (-0.5),
        FF ** (-0.5),
    ]
    pieces = []
    for (row_total, col_total), rate_value in zip(matrix_shapes(), rate_list):
        tile_count = row_total // band_total // BLK * (col_total // BLK)
        pieces.append(jnp.full((tile_count,), rate_value, jnp.float32))
    return jnp.concatenate(pieces)


def band_matrices(tiles, band_total):
    matrices = []
    offset = 0
    for row_total, col_total in matrix_shapes():
        band_rows = row_total // band_total
        tile_count = band_rows // BLK * (col_total // BLK)
        segment = tiles[offset : offset + tile_count].reshape(
            band_rows // BLK, col_total // BLK, BLK, BLK
        )
        matrices.append(segment.transpose(0, 2, 1, 3).reshape(band_rows, col_total))
        offset += tile_count
    return matrices


def band_tiles(matrices):
    pieces = []
    for matrix in matrices:
        row_count, col_count = matrix.shape
        segment = matrix.reshape(row_count // BLK, BLK, col_count // BLK, BLK).transpose(0, 2, 1, 3)
        pieces.append(segment.reshape(-1, BLK, BLK))
    return jnp.concatenate(pieces, 0)


def rope_tables(position):
    halves = jnp.arange(HD // 2, dtype=jnp.float32) * (2.0 / HD)
    frequency = rope_theta ** (-halves)
    angles = position.astype(jnp.float32)[:, None] * frequency[None, :]
    angles = jnp.concatenate([angles, angles], 1)
    return (jnp.cos(angles), jnp.sin(angles))


def rotate(vectors, cosine_table, sine_table):
    half_width = vectors.shape[-1] // 2
    turned = jnp.concatenate([-vectors[..., half_width:], vectors[..., :half_width]], -1)
    return vectors * cosine_table[:, None, :] + turned * sine_table[:, None, :]


def rotate_back(grad_rows, cosine_table, sine_table):
    half_width = grad_rows.shape[-1] // 2
    scaled = grad_rows * sine_table[:, None, :]
    turned = jnp.concatenate([scaled[..., half_width:], -scaled[..., :half_width]], -1)
    return grad_rows * cosine_table[:, None, :] + turned


def norm_back(values, row_scale, gain_row, grad_rows):
    weighted = grad_rows * gain_row
    return row_scale * weighted - values * row_scale**3 * jnp.mean(
        weighted * values, -1, keepdims=True
    )


def to_rep(block, distance):
    route = [(i, i ^ distance) for i in range(lax.axis_size("rep"))]
    return lax.ppermute(block, "rep", route)


def square():
    return lax.axis_size("rep") == 4


def gather_first(block):
    if not square():
        return (lax.all_gather(block, "rep", axis=0),)
    return block, to_rep(block, 1), to_rep(block, 2)


def gather_second(first):
    if not square():
        return first
    block, near, far = first
    cut = block.shape[0] // 2
    return block, near, far, to_rep(near[:cut], 2), to_rep(far[cut:], 1)


def gather_join(pieces):
    if not square():
        return pieces[0]
    return jnp.concatenate(pieces, 0).reshape((4,) + pieces[0].shape)


def square_pieces(block):
    return gather_second(gather_first(block))


def rep_gather(block):
    return gather_join(gather_second(gather_first(block)))


def after(values, *others):
    count = len(values)
    tied = lax.optimization_barrier((*values, *others))
    return tuple(tied[:count]), *tied[count:]


def rep_of(entry):
    place = lax.axis_index("rep")
    return place ^ entry if square() else entry


def rep_scatter(parts):
    if not square():
        flat = parts.reshape(-1, parts.shape[-1])
        return lax.psum_scatter(flat, "rep", scatter_dimension=0, tiled=True).astype(jnp.float32)
    return sum_pieces(*split_pieces(parts))


def split_pieces(parts):
    half = parts.shape[-1] // 2
    low, high = parts[..., :half], parts[..., half:]
    return jnp.stack([low[0], low[2]], 0), jnp.stack([low[1], low[3]], 0), high[:2], high[2:]


def sum_first(pieces):
    low_kept, low_sent, high_kept, high_sent = pieces
    parts = []
    for kept, sent, first in ((low_kept, low_sent, 1), (high_kept, high_sent, 2)):
        came = to_rep(sent, first)
        parts.append(kept[0].astype(jnp.float32) + came[0].astype(jnp.float32))
        parts.append((kept[1].astype(jnp.float32) + came[1].astype(jnp.float32)).astype(kept.dtype))
    return tuple(parts)


def sum_second(parts):
    low, low_other, high, high_other = parts
    low = low + to_rep(low_other, 2).astype(jnp.float32)
    high = high + to_rep(high_other, 1).astype(jnp.float32)
    return jnp.concatenate([low, high], -1)


def sum_pieces(*pieces):
    return sum_second(sum_first(pieces))


def add_all(value, axis, distance=1):
    size = lax.axis_size(axis)
    total = value.astype(jnp.float32)
    while distance < size:
        count = 2 if (size // distance).bit_length() % 2 == 0 else 4
        low = total.astype(value.dtype)
        others = []
        for step in range(1, count):
            route = [(i, i ^ (step * distance)) for i in range(size)]
            others.append(lax.ppermute(low, axis, route).astype(jnp.float32))
        total = total + others[0]
        if count == 4:
            total = total + (others[1] + others[2])
        distance *= count
    return total


def rep_features(block):
    if not square():
        return lax.all_gather(block, "rep", axis=2, tiled=True)
    own, near, far, low, high = square_pieces(block)
    return jnp.concatenate(
        [
            own,
            jnp.stack([near[1], near[0], near[3], near[2]], 0),
            jnp.stack([far[2], far[3], far[0], far[1]], 0),
            jnp.stack([high[1], high[0], low[1], low[0]], 0),
        ],
        2,
    )


def write_pieces(entry, rows, values, refs):
    low_kept, low_sent, high_kept, high_sent = refs
    half = low_kept.shape[-1]
    values = values.astype(jnp.bfloat16)
    (low_sent if entry % 2 else low_kept)[entry // 2, rows] = values[:, :half]
    (high_sent if entry // 2 else high_kept)[entry % 2, rows] = values[:, half:]


def swapped_kernel(x_ref, w_ref, *refs):
    reps, rows, _ = x_ref.shape
    width = w_ref.shape[0] // reps
    for entry in range(reps):
        weight = w_ref[entry * width : (entry + 1) * width]
        for there in range(reps):
            product = over_last(x_ref[there ^ entry], weight)
            write_pieces(entry, slice(there * rows, (there + 1) * rows), product, refs)


def rep_features_sum(columns, weight, meanwhile):
    reps, rows, depth = columns.shape
    width = weight.shape[0] // reps
    if square():
        pieces = pl.pallas_call(
            swapped_kernel,
            out_shape=[jax.ShapeDtypeStruct((2, reps * rows, width // 2), jnp.bfloat16)] * 4,
            compiler_params=pltpu.CompilerParams(vmem_limit_bytes=32 * 2**20),
            cost_estimate=pl.CostEstimate(
                flops=2 * reps * columns.size * width,
                bytes_accessed=10 * columns.size,
                transcendentals=0,
            ),
        )(columns, weight)
        first = sum_first(pieces)
        first, other = after(first, meanwhile())
        total = sum_second(first)
    else:
        other = meanwhile()
        product = over_last(columns.reshape(-1, depth), weight).astype(jnp.bfloat16)
        swapped = product.reshape(reps, rows, reps, width).transpose(2, 0, 1, 3)
        total = rep_scatter(swapped.reshape(reps, reps * rows, width))
    return total.reshape(reps, rows, width), other


def rep_exchange(parts):
    if not square():
        return lax.all_to_all(parts, "rep", 0, 0)
    return jnp.stack([parts[0]] + [to_rep(parts[entry], entry) for entry in (1, 2, 3)], 0)


def by_place(parts):
    entries = [rep_of(entry) for entry in range(parts.shape[0])]
    return jnp.stack([lax.dynamic_index_in_dim(parts, entry, 0, False) for entry in entries], 0)


def to_core(block):
    return lax.ppermute(block, "fsdp", [(i, i ^ 1) for i in range(lax.axis_size("fsdp"))])


def shifted(block, axis, distance):
    devices = range(lax.axis_size(axis))
    route = [(i - distance, i) for i in devices if i - distance in devices]
    return lax.ppermute(block, axis, route)


def tile_offsets(band_total):
    offsets = [0]
    for row_total, col_total in matrix_shapes():
        offsets.append(offsets[-1] + row_total // band_total // BLK * (col_total // BLK))
    return offsets


def whole_tiles(band_total, rep_total):
    return KVH * HD // rep_total % BLK == 0 and FF // band_total // rep_total % BLK == 0


def slice_layout(band_total, rep_total):
    offsets = tile_offsets(band_total)
    layout = []
    for kind, (row_total, col_total) in enumerate(matrix_shapes()):
        rows, cols = row_total // band_total // BLK, col_total // BLK
        grid = offsets[kind] + np.arange(rows * cols).reshape(rows, cols)
        if kind == 6:
            layout.append(grid.reshape(rep_total, rows // rep_total, cols))
        elif kind in (4, 5):
            cut = grid.reshape(rows, band_total, rep_total, -1).transpose(2, 0, 1, 3)
            layout.append(cut.reshape(rep_total, rows, -1))
        else:
            layout.append(grid.reshape(rows, rep_total, -1).transpose(1, 0, 2))
    return layout


def tiles_to_matrix(tiles):
    rows, cols = tiles.shape[:2]
    return tiles.transpose(0, 2, 1, 3).reshape(rows * BLK, cols * BLK)


def matrix_to_tiles(matrix):
    rows, cols = matrix.shape
    cut = matrix.reshape(rows // BLK, BLK, cols // BLK, BLK)
    return cut.transpose(0, 2, 1, 3).reshape(-1, BLK, BLK)


def cut_slices(matrices, band_total, rep_total):
    place = lax.axis_index("rep")
    slices = []
    for kind, matrix in enumerate(matrices):
        rows, cols = matrix.shape
        if kind == 6:
            slices.append(lax.dynamic_slice_in_dim(matrix, place * (rows // rep_total), rows // rep_total, 0))
        elif kind in (4, 5):
            cut = matrix.reshape(rows, band_total, rep_total, -1)
            slices.append(lax.dynamic_index_in_dim(cut, place, 2, False).reshape(rows, -1))
        else:
            slices.append(lax.dynamic_slice_in_dim(matrix, place * (cols // rep_total), cols // rep_total, 1))
    return slices


def join_slices(stacks, band_total, rep_total):
    matrices = []
    for kind, stack in enumerate(stacks):
        rows, cols = stack.shape[1:]
        if kind == 6:
            matrices.append(stack.reshape(-1, cols))
        elif kind in (4, 5):
            cut = stack.reshape(rep_total, rows, band_total, -1).transpose(1, 2, 0, 3)
            matrices.append(cut.reshape(rows, -1))
        else:
            matrices.append(stack.transpose(1, 0, 2).reshape(rows, -1))
    return matrices


def gather_kernel(grids, meta, *refs):
    source_total = len(refs) - len(grids) - 1
    sources, targets, done = refs[:source_total], refs[source_total:-1], refs[-1]
    height = sources[0].shape[1]
    start = 0
    for place, (target, (rows, cols)) in enumerate(zip(targets, grids)):

        def one(tile, carry, target=target, rows=rows, cols=cols, start=start, place=place):
            kind = meta[0, start + tile]
            row = meta[1, start + tile]
            across = tile % cols
            top = pl.multiple_of((across // 2 * rows + tile // cols) * height, height)
            left = pl.multiple_of(across % 2 * BLK, BLK)
            for number, source in enumerate(sources):

                @pl.when(kind == number)
                def _(source=source):
                    pltpu.make_async_copy(
                        source.at[row], target.at[pl.ds(top, height), pl.ds(left, BLK)], done.at[place]
                    ).start()

            return carry

        lax.fori_loop(0, rows * cols, one, 0)
        start += rows * cols
    for place, target in enumerate(targets):
        pltpu.make_async_copy(target, target, done.at[place]).wait()


def gather_strips(sources, meta, grids):
    anywhere = pl.BlockSpec(memory_space=pl.ANY)
    height = sources[0].shape[1]
    out_shape = [
        jax.ShapeDtypeStruct((cols // 2 * rows * height, 2 * BLK), jnp.bfloat16) for rows, cols in grids
    ]
    return pl.pallas_call(
        functools.partial(gather_kernel, grids),
        out_shape=out_shape,
        grid_spec=pltpu.PrefetchScalarGridSpec(
            num_scalar_prefetch=1,
            grid=(1,),
            in_specs=[anywhere] * len(sources),
            out_specs=[pl.BlockSpec(shape.shape, lambda i, *_: (0, 0)) for shape in out_shape],
            scratch_shapes=[pltpu.SemaphoreType.DMA((len(grids),))],
        ),
        compiler_params=pltpu.CompilerParams(vmem_limit_bytes=32 * 2**20),
        cost_estimate=pl.CostEstimate(
            flops=0, bytes_accessed=sum(4 * shape.size for shape in out_shape), transcendentals=0
        ),
    )(meta, *sources)


def place_kernel(entries, rows, cols, meta, low, high, out_ref, done):
    out_ref[...] = jnp.zeros_like(out_ref)
    height = low.shape[1]

    def copies(tile):
        entry, rest = tile // (rows * cols), tile % (rows * cols)
        top = rest // cols * (2 * height)
        left = pl.multiple_of(rest % cols * BLK, BLK)
        return [
            pltpu.make_async_copy(
                half.at[meta[1, tile]],
                out_ref.at[entry, pl.ds(pl.multiple_of(top + part * height, height), height), pl.ds(left, BLK)],
                done.at[part],
            )
            for part, half in enumerate((low, high))
        ]

    def begin(tile, carry):
        @pl.when(meta[0, tile] == 1)
        def _():
            for copy in copies(tile):
                copy.start()

        return carry

    def finish(tile, carry):
        @pl.when(meta[0, tile] == 1)
        def _():
            for copy in copies(tile):
                copy.wait()

        return carry

    lax.fori_loop(0, entries * rows * cols, begin, 0)
    lax.fori_loop(0, entries * rows * cols, finish, 0)


def place_tiles(low, high, meta, entries, rows, cols):
    shape = (entries, rows * BLK, cols * BLK)
    anywhere = pl.BlockSpec(memory_space=pl.ANY)
    return pl.pallas_call(
        functools.partial(place_kernel, entries, rows, cols),
        out_shape=jax.ShapeDtypeStruct(shape, jnp.bfloat16),
        grid_spec=pltpu.PrefetchScalarGridSpec(
            num_scalar_prefetch=1,
            grid=(1,),
            in_specs=[anywhere, anywhere],
            out_specs=pl.BlockSpec(shape, lambda i, *_: (0, 0, 0)),
            scratch_shapes=[pltpu.SemaphoreType.DMA((2,))],
        ),
        compiler_params=pltpu.CompilerParams(vmem_limit_bytes=32 * 2**20),
        cost_estimate=pl.CostEstimate(
            flops=0, bytes_accessed=4 * entries * rows * cols * BLK * BLK, transcendentals=0
        ),
    )(meta, low, high)


def half_turn(values):
    lane = lax.broadcasted_iota(jnp.int32, values.shape, 1)
    lanes = values.shape[1]
    first = lane % HD < HD // 2
    return first, jnp.where(
        first, pltpu.roll(values, lanes - HD // 2, 1), pltpu.roll(values, HD // 2, 1)
    )


def strip_copies(early, late, target, done):
    return [
        pltpu.make_async_copy(half, target.at[:, :, number], done.at[number])
        for number, half in enumerate((early, late))
    ]


def forward_kernel(x_ref, early, late, gate_ref, up_ref, act_ref, weights, done):
    step, steps = pl.program_id(0), pl.num_programs(0)
    slot = step % 2
    width = weights.shape[-1]

    def copies(number, at_step, at_slot):
        strip = number * steps + at_step
        return strip_copies(
            early.at[:, strip], late.at[:, strip], weights.at[number, at_slot], done.at[number, at_slot]
        )

    def fetch(at_step, at_slot):
        for number in range(2):
            for copy in copies(number, at_step, at_slot):
                copy.start()

    @pl.when(step == 0)
    def _():
        fetch(0, 0)

    @pl.when(step + 1 < steps)
    def _():
        fetch(step + 1, 1 - slot)

    for number in range(2):
        for copy in copies(number, step, slot):
            copy.wait()
    gate_weight, up_weight = (weights[number, slot].reshape(-1, width) for number in range(2))
    chunk = min(2 * BLK, x_ref.shape[0])
    for first in range(0, x_ref.shape[0], chunk):
        rows = slice(first, first + chunk)
        gate = jnp.dot(x_ref[rows], gate_weight, preferred_element_type=jnp.float32)
        up = jnp.dot(x_ref[rows], up_weight, preferred_element_type=jnp.float32)
        gate_ref[rows] = gate.astype(jnp.bfloat16)
        up_ref[rows] = up.astype(jnp.bfloat16)
        act_ref[rows] = (gate * jax.nn.sigmoid(gate) * up).astype(jnp.bfloat16)


def forward_products(rows, early, late, columns):
    tokens, depth = rows.shape
    bands, _, tiles, half, width = early.shape
    block = pl.BlockSpec((tokens, width), lambda n: (0, n))
    anywhere = pl.BlockSpec(memory_space=pl.ANY)
    return pl.pallas_call(
        forward_kernel,
        out_shape=[jax.ShapeDtypeStruct((tokens, columns), jnp.bfloat16)] * 3,
        grid=(columns // width,),
        in_specs=[pl.BlockSpec(rows.shape, lambda n: (0, 0)), anywhere, anywhere],
        out_specs=[block] * 3,
        scratch_shapes=[
            pltpu.VMEM((2, 2, bands, tiles, 2, half, width), jnp.bfloat16),
            pltpu.SemaphoreType.DMA((2, 2, 2)),
        ],
        compiler_params=pltpu.CompilerParams(vmem_limit_bytes=48 * 2**20),
        cost_estimate=pl.CostEstimate(
            flops=tokens * depth * columns // 8, bytes_accessed=2 * rows.size, transcendentals=0
        ),
    )(rows, early, late)


def backward_kernel(top_ref, gate_ref, up_ref, act_ref, early, late, late_down, *refs):
    dgate_ref, dup_ref = refs[:2]
    pieces, branch_pieces = refs[2:6], refs[6:10]
    weights, downs, total, branch, done, down_done = refs[10:]
    step, steps = pl.program_id(0), pl.num_programs(0)
    slot = step % 2
    strips, width = downs.shape[1], downs.shape[-1]

    def down_copies(at_step, at_slot):
        wanted = pl.ds(2 * steps, strips)
        return strip_copies(
            early.at[at_step, wanted], late_down.at[at_step], downs.at[at_slot], down_done.at[at_slot]
        )

    def copies(number, at_step, at_slot):
        strip = number * steps + at_step
        return strip_copies(
            early.at[:, strip], late.at[:, strip], weights.at[number, at_slot], done.at[number, at_slot]
        )

    def fetch(at_step, at_slot):
        for copy in down_copies(at_step, at_slot):
            copy.start()
        for number in range(2):
            for copy in copies(number, at_step, at_slot):
                copy.start()

    @pl.when(step == 0)
    def _():
        fetch(0, 0)
        total[...] = jnp.zeros_like(total)
        branch[...] = jnp.zeros_like(branch)

    @pl.when(step + 1 < steps)
    def _():
        fetch(step + 1, 1 - slot)

    for copy in down_copies(step, slot):
        copy.wait()
    for number in range(2):
        for copy in copies(number, step, slot):
            copy.wait()
    gate_weight, up_weight = (weights[number, slot].reshape(-1, width) for number in range(2))
    chunk = min(4 * BLK, top_ref.shape[0])
    for first in range(0, top_ref.shape[0], chunk):
        rows = slice(first, first + chunk)
        grad_act = 0.0
        for strip in range(strips):
            lanes = slice(strip * width, (strip + 1) * width)
            down = downs[slot, strip].reshape(-1, width)
            grad_act = grad_act + over_last(top_ref[rows, lanes], down)
            branch[rows, lanes] += jnp.dot(act_ref[rows], down, preferred_element_type=jnp.float32)
        gate = gate_ref[rows].astype(jnp.float32)
        up = up_ref[rows].astype(jnp.float32)
        sigmoid_gate = jax.nn.sigmoid(gate)
        grad_gate = grad_act * up * sigmoid_gate * (1.0 + gate * (1.0 - sigmoid_gate))
        grad_gate = grad_gate.astype(jnp.bfloat16)
        grad_up = (grad_act * (gate * sigmoid_gate)).astype(jnp.bfloat16)
        dgate_ref[rows] = grad_gate
        dup_ref[rows] = grad_up
        total[rows] += over_last(grad_gate, gate_weight) + over_last(grad_up, up_weight)

    @pl.when(step == steps - 1)
    def _():
        rows = total.shape[0] // 4
        for entry in range(4):
            part = slice(entry * rows, (entry + 1) * rows)
            write_pieces(entry, slice(0, rows), total[part], pieces)
            write_pieces(entry, slice(0, rows), branch[part], branch_pieces)


def backward_products(top, gate, up, act, early, late, late_down):
    tokens, depth = top.shape
    columns = gate.shape[1]
    bands, _, tiles, half, width = early.shape
    strips = depth // width
    block = pl.BlockSpec((tokens, width), lambda n: (0, n))
    anywhere = pl.BlockSpec(memory_space=pl.ANY)
    piece = jax.ShapeDtypeStruct((2, tokens // 4, depth // 2), jnp.bfloat16)
    grads = jax.ShapeDtypeStruct((tokens, columns), jnp.bfloat16)
    outs = pl.pallas_call(
        backward_kernel,
        out_shape=[grads] * 2 + [piece] * 8,
        grid=(columns // width,),
        in_specs=[pl.BlockSpec(top.shape, lambda n: (0, 0))] + [block] * 3 + [anywhere] * 3,
        out_specs=[block] * 2 + [pl.BlockSpec(piece.shape, lambda n: (0, 0, 0))] * 8,
        scratch_shapes=[
            pltpu.VMEM((2, 2, bands, tiles, 2, half, width), jnp.bfloat16),
            pltpu.VMEM((2, strips, tiles, 2, half, width), jnp.bfloat16),
            pltpu.VMEM((tokens, depth), jnp.float32),
            pltpu.VMEM((tokens, depth), jnp.float32),
            pltpu.SemaphoreType.DMA((2, 2, 2)),
            pltpu.SemaphoreType.DMA((2, 2)),
        ],
        compiler_params=pltpu.CompilerParams(vmem_limit_bytes=60 * 2**20),
        cost_estimate=pl.CostEstimate(
            flops=8 * tokens * depth * columns, bytes_accessed=8 * columns * depth, transcendentals=0
        ),
    )(top, gate, up, act, early, late, late_down)
    return outs[0], outs[1], outs[2:6], outs[6:10]


def rope_kernel(q_width, kv_width, x_ref, cos_ref, sin_ref, *outs):
    width = x_ref.shape[-1]
    for start in range(0, width, BLK):
        values = x_ref[0, :, start : start + BLK]
        first, turned = half_turn(values)
        sines = sin_ref[0]
        turned_rows = values * cos_ref[0] + turned * jnp.where(first, -sines, sines)
        if start + BLK > q_width + kv_width:
            column = lax.broadcasted_iota(jnp.int32, values.shape, 1) + start
            turned_rows = jnp.where(column >= q_width + kv_width, values, turned_rows)
        if start < q_width:
            outs[0][0, :, start : start + BLK] = (turned_rows * HD ** (-0.5)).astype(jnp.bfloat16)
        else:
            outs[-1][0, :, start - q_width : start - q_width + BLK] = turned_rows.astype(jnp.bfloat16)


def rope_rows(inner, rows, row_block, q_width, kv_width, cosines, sines, with_queries=True):
    seqs, _, width = inner.shape
    shared = cosines.shape[0] == 1
    table = pl.BlockSpec((1, rows, BLK), lambda s: (0 if shared else s, 0, 0))
    widths = [q_width, 2 * kv_width]
    column_block = 0
    if not with_queries:
        width, column_block = 2 * kv_width, q_width // (2 * kv_width)
        widths, q_width = widths[1:], 0
    return pl.pallas_call(
        functools.partial(rope_kernel, q_width, kv_width),
        out_shape=[jax.ShapeDtypeStruct((seqs, rows, w), jnp.bfloat16) for w in widths],
        grid=(seqs,),
        in_specs=[pl.BlockSpec((1, rows, width), lambda s: (s, row_block, column_block)), table, table],
        out_specs=[pl.BlockSpec((1, rows, w), lambda s: (s, 0, 0)) for w in widths],
        cost_estimate=pl.CostEstimate(
            flops=6 * seqs * rows * width, bytes_accessed=6 * seqs * rows * width, transcendentals=0
        ),
    )(inner, cosines, sines)


def fill_bias(band_ref, gpos_ref, bias_ref, rows, window_len):
    band = band_ref[0]

    @pl.when(pl.program_id(0) == 0)
    def _():
        key = lax.broadcasted_iota(jnp.int32, (window_len, rows), 0) + (
            band * rows - (window_len - rows)
        )
        query = lax.broadcasted_iota(jnp.int32, (window_len, rows), 1) + band * rows
        inside = (key > query - WINDOW) & (key <= query) & (key >= 0)
        bias_ref[:window_len] = jnp.where(inside, 0.0, masked_value)

    glob_total = gpos_ref.shape[1]
    query = lax.broadcasted_iota(jnp.int32, (glob_total, rows), 1) + (band * rows - WINDOW)
    spot = jnp.broadcast_to(gpos_ref[0][:, :1], (glob_total, rows))
    bias_ref[window_len:] = jnp.where(spot <= query.astype(jnp.float32), 0.0, masked_value)


def over_last(left, right):
    return lax.dot_general(left, right, (((1,), (1,)), ((), ())), preferred_element_type=jnp.float32)


def over_first(left, right):
    return lax.dot_general(left, right, (((0,), (0,)), ((), ())), preferred_element_type=jnp.float32)


def attend_kernel(block_total, band_ref, gpos_ref, q_ref, *refs):
    blocks, (out_ref, lse_ref, bias_ref) = refs[:block_total], refs[block_total:]
    rows, q_width = q_ref.shape[1:]
    kv_width = blocks[0].shape[2] // 2
    heads, group = q_width // HD, q_width // kv_width
    window_len = rows * (block_total - 1)
    fill_bias(band_ref, gpos_ref, bias_ref, rows, window_len)
    starts = [rows * number for number in range(block_total)]
    pending = []
    for head in range(heads):
        left = head // group * HD
        queries = q_ref[0, :, head * HD : (head + 1) * HD]
        scores = [
            over_last(block[0, :, left : left + HD], queries)
            + bias_ref[start : start + block.shape[1]]
            for block, start in zip(blocks, starts)
        ]
        top = functools.reduce(jnp.maximum, [jnp.max(part, 0, keepdims=True) for part in scores])
        total = 0.0
        mixed = 0.0
        for block, part in zip(blocks, scores):
            weights = jnp.exp(part - top)
            total = total + jnp.sum(weights, 0, keepdims=True)
            mixed = mixed + over_first(
                block[0, :, kv_width + left : kv_width + left + HD], weights.astype(jnp.bfloat16)
            )
        lse_ref[0, head : head + 1, :] = top + jnp.log(total)
        pending.append(mixed / total)
        if len(pending) * HD == BLK or head == heads - 1:
            stop = (head + 1) * HD
            both = jnp.concatenate(pending, 0).T
            out_ref[0, :, stop - both.shape[1] : stop] = both.astype(jnp.bfloat16)
            pending = []


def attend(band, gpos, queries, blocks):
    seqs, rows, q_width = queries.shape
    heads = q_width // HD
    key_total = sum(block.shape[1] for block in blocks)

    def whole(array):
        return pl.BlockSpec((1,) + array.shape[1:], lambda s, *_: (s, 0, 0))

    out_shape = [
        jax.ShapeDtypeStruct((seqs, rows, q_width), jnp.bfloat16),
        jax.ShapeDtypeStruct((seqs, heads, rows), jnp.float32),
    ]
    return pl.pallas_call(
        functools.partial(attend_kernel, len(blocks)),
        out_shape=out_shape,
        grid_spec=pltpu.PrefetchScalarGridSpec(
            num_scalar_prefetch=1,
            grid=(seqs,),
            in_specs=[whole(array) for array in (gpos, queries, *blocks)],
            out_specs=[whole(array) for array in out_shape],
            scratch_shapes=[pltpu.VMEM((key_total, rows), jnp.float32)],
        ),
        compiler_params=pltpu.CompilerParams(vmem_limit_bytes=48 * 2**20),
        cost_estimate=pl.CostEstimate(
            flops=16 * seqs * heads * rows * key_total * HD,
            bytes_accessed=4 * queries.size,
            transcendentals=seqs * heads * rows * key_total,
        ),
    )(band, gpos, queries, *blocks)


def attend_back_kernel(block_total, band_ref, gpos_ref, cos_ref, sin_ref, q_ref, grad_ref, lse_ref, *refs):
    blocks = refs[:block_total]
    dq_ref = refs[block_total]
    out_refs = refs[block_total + 1 : 2 * block_total + 1]
    bias_ref = refs[-1]
    rows, q_width = q_ref.shape[1:]
    kv_width = blocks[0].shape[2] // 2
    heads, group = q_width // HD, q_width // kv_width
    window_len = rows * (block_total - 1)
    fill_bias(band_ref, gpos_ref, bias_ref, rows, window_len)
    starts = [rows * number for number in range(block_total)]
    pending = []
    for kv_head in range(kv_width // HD):
        left = kv_head * HD
        key_sums = [0.0] * block_total
        value_sums = [0.0] * block_total
        for head in range(kv_head * group, (kv_head + 1) * group):
            queries = q_ref[0, :, head * HD : (head + 1) * HD]
            grads = grad_ref[0, :, head * HD : (head + 1) * HD]
            lse = lse_ref[0, head : head + 1, :]
            soft, soft_grads = [], []
            inner = 0.0
            for number, (block, start) in enumerate(zip(blocks, starts)):
                part = over_last(block[0, :, left : left + HD], queries)
                part = jnp.exp(part + bias_ref[start : start + block.shape[1]] - lse)
                slope = over_last(block[0, :, kv_width + left : kv_width + left + HD], grads)
                inner = inner + jnp.sum(part * slope, 0, keepdims=True)
                soft.append(part)
                soft_grads.append(slope)
            turned = 0.0
            for number, block in enumerate(blocks):
                score_grads = (soft[number] * (soft_grads[number] - inner)).astype(jnp.bfloat16)
                value_sums[number] = value_sums[number] + jnp.dot(
                    soft[number].astype(jnp.bfloat16), grads, preferred_element_type=jnp.float32
                )
                key_sums[number] = key_sums[number] + jnp.dot(
                    score_grads, queries, preferred_element_type=jnp.float32
                )
                turned = turned + over_first(block[0, :, left : left + HD], score_grads)
            pending.append(turned)
            if len(pending) * HD == BLK or head == heads - 1:
                stop = (head + 1) * HD
                both = jnp.concatenate(pending, 0).T * HD ** (-0.5)
                pending = []
                first, other = half_turn(both * sin_ref[0])
                both = both * cos_ref[0] + jnp.where(first, other, -other)
                dq_ref[0, :, stop - both.shape[1] : stop] = both.astype(jnp.bfloat16)
        for number, out_ref in enumerate(out_refs):
            out_ref[0, :, left : left + HD] = key_sums[number].astype(out_ref.dtype)
            out_ref[0, :, kv_width + left : kv_width + left + HD] = value_sums[number].astype(
                out_ref.dtype
            )


def attend_back(band, gpos, cosines, sines, queries, grads, lse, blocks):
    seqs, rows, q_width = queries.shape
    heads = q_width // HD
    key_total = sum(block.shape[1] for block in blocks)

    def whole(array):
        return pl.BlockSpec((1,) + array.shape[1:], lambda s, *_: (s, 0, 0))

    table = pl.BlockSpec((1, rows, BLK), lambda s, *_: (0, 0, 0))
    out_shape = [jax.ShapeDtypeStruct(queries.shape, jnp.bfloat16)]
    for number, block in enumerate(blocks):
        own = number == len(blocks) - 2
        out_shape.append(jax.ShapeDtypeStruct(block.shape, jnp.float32 if own else jnp.bfloat16))
    return pl.pallas_call(
        functools.partial(attend_back_kernel, len(blocks)),
        out_shape=out_shape,
        grid_spec=pltpu.PrefetchScalarGridSpec(
            num_scalar_prefetch=1,
            grid=(seqs,),
            in_specs=[whole(gpos), table, table]
            + [whole(array) for array in (queries, grads, lse, *blocks)],
            out_specs=[whole(array) for array in out_shape],
            scratch_shapes=[pltpu.VMEM((key_total, rows), jnp.float32)],
        ),
        compiler_params=pltpu.CompilerParams(vmem_limit_bytes=48 * 2**20),
        cost_estimate=pl.CostEstimate(
            flops=40 * seqs * heads * rows * key_total * HD,
            bytes_accessed=8 * queries.size,
            transcendentals=seqs * heads * rows * key_total,
        ),
    )(band, gpos, cosines, sines, queries, grads, lse, *blocks)


def join_kernel(q_width, kv_width, dq_ref, own_ref, pick_ref, glob_ref, cos_ref, sin_ref, *refs):
    back_refs, out_ref = refs[:-1], refs[-1]
    out_ref[0, :, :q_width] = dq_ref[0]
    picked = lax.dot_general(
        pick_ref[0].astype(jnp.float32),
        glob_ref[0],
        (((0,), (0,)), ((), ())),
        precision=lax.Precision.HIGHEST,
        preferred_element_type=jnp.float32,
    )
    for start in range(0, 2 * kv_width, BLK):
        lanes = slice(start, start + BLK)
        total = own_ref[0, :, lanes] + picked[:, lanes]
        for back_ref in back_refs:
            total = total + back_ref[0, :, lanes].astype(jnp.float32)
        first, other = half_turn(total * sin_ref[0])
        turned = total * cos_ref[0] + jnp.where(first, other, -other)
        column = lax.broadcasted_iota(jnp.int32, total.shape, 1) + start
        turned = jnp.where(column >= kv_width, total, turned)
        out_ref[0, :, q_width + start : q_width + start + BLK] = turned.astype(jnp.bfloat16)


def join_grads(dq, own, picks, globs, cosines, sines, backs):
    seqs, rows, q_width = dq.shape
    kv_width = own.shape[2] // 2

    def whole(array):
        return pl.BlockSpec((1,) + array.shape[1:], lambda s: (s, 0, 0))

    table = pl.BlockSpec((1, rows, BLK), lambda s: (0, 0, 0))
    out_shape = jax.ShapeDtypeStruct((seqs, rows, q_width + 2 * kv_width), jnp.bfloat16)
    return pl.pallas_call(
        functools.partial(join_kernel, q_width, kv_width),
        out_shape=out_shape,
        grid=(seqs,),
        in_specs=[whole(dq), whole(own), whole(picks), whole(globs), table, table]
        + [whole(back) for back in backs],
        out_specs=whole(out_shape),
        cost_estimate=pl.CostEstimate(
            flops=20 * own.size, bytes_accessed=4 * dq.size + 12 * own.size, transcendentals=0
        ),
    )(dq, own, picks, globs, cosines, sines, *backs)


def adam_kernel(batch, meta, rates, *refs):
    master_ref, first_ref, second_ref, left_ref, right_ref = refs[:5]
    sources = refs[5:-6]
    new_first_ref, new_second_ref, new_master_ref, copy_ref, tiles, arrived = refs[-6:]
    step, steps = pl.program_id(0), pl.num_programs(0)
    slot = step % 2

    def fetch(at_step, at_slot):
        for place in range(batch):
            tile = at_step * batch + place
            for number, source in enumerate(sources):

                @pl.when(meta[0, tile] == number)
                def _(source=source, tile=tile, place=place):
                    top = pl.multiple_of(meta[2, tile], BLK)
                    left = pl.multiple_of(meta[3, tile], BLK)
                    pltpu.make_async_copy(
                        source.at[meta[1, tile], pl.ds(top, BLK), pl.ds(left, BLK)],
                        tiles.at[at_slot, place],
                        arrived.at[at_slot],
                    ).start()

    @pl.when(step == 0)
    def _():
        fetch(0, 0)

    @pl.when(step + 1 < steps)
    def _():
        fetch(step + 1, 1 - slot)

    pltpu.make_async_copy(tiles.at[slot], tiles.at[slot], arrived.at[slot]).wait()
    places = range(batch)
    lefts = [left_ref[place].astype(jnp.bfloat16) for place in places]
    rights = [right_ref[place].astype(jnp.bfloat16) for place in places]
    turned = [over_first(lefts[place], tiles[slot, place]).astype(jnp.bfloat16) for place in places]
    rotated = [
        jnp.dot(turned[place], rights[place], preferred_element_type=jnp.float32) for place in places
    ]
    directions = []
    for place in places:
        new_first = beta_one * first_ref[place] + (1.0 - beta_one) * rotated[place]
        new_second = beta_two * second_ref[place] + (1.0 - beta_two) * rotated[place] * rotated[place]
        direction = (new_first * (1.0 / (1.0 - beta_one**STEP))) / (
            jnp.sqrt(new_second * (1.0 / (1.0 - beta_two**STEP))) + adam_eps
        )
        new_first_ref[place] = new_first
        new_second_ref[place] = new_second
        directions.append(direction.astype(jnp.bfloat16))
    updates = [
        jnp.dot(lefts[place], directions[place], preferred_element_type=jnp.float32) for place in places
    ]
    updates = [over_last(updates[place].astype(jnp.bfloat16), rights[place]) for place in places]
    for place in places:
        old = master_ref[place]
        new_master = old - rates[step * batch + place] * (updates[place] + weight_decay * old)
        new_master_ref[place] = new_master
        copy_ref[place] = new_master.astype(jnp.bfloat16)


def adam(meta, rates, state, sources):
    count = state[0].shape[0]
    batch = max(size for size in range(1, 33) if count % size == 0)
    block = pl.BlockSpec((batch, BLK, BLK), lambda s, *_: (s, 0, 0))
    anywhere = pl.BlockSpec(memory_space=pl.ANY)
    shape = (count, BLK, BLK)
    return pl.pallas_call(
        functools.partial(adam_kernel, batch),
        out_shape=[jax.ShapeDtypeStruct(shape, jnp.float32)] * 3
        + [jax.ShapeDtypeStruct(shape, jnp.bfloat16)],
        grid_spec=pltpu.PrefetchScalarGridSpec(
            num_scalar_prefetch=2,
            grid=(count // batch,),
            in_specs=[block] * 5 + [anywhere] * len(sources),
            out_specs=[block] * 4,
            scratch_shapes=[
                pltpu.VMEM((2, batch, BLK, BLK), jnp.bfloat16),
                pltpu.SemaphoreType.DMA((2,)),
            ],
        ),
        compiler_params=pltpu.CompilerParams(vmem_limit_bytes=56 * 2**20),
        cost_estimate=pl.CostEstimate(
            flops=8 * count * BLK**3, bytes_accessed=36 * count * BLK**2, transcendentals=0
        ),
    )(meta, rates, *state, *sources)


def per_device(
    block_input,
    cotangent,
    glob_select,
    assignment,
    master,
    first_moment,
    second_moment,
    left_basis,
    right_basis,
    gains,
    gain_first,
    gain_second,
):
    band_total = lax.axis_size("fsdp")
    rep_total = lax.axis_size("rep")
    place = lax.axis_index("rep")
    band = lax.axis_index("fsdp")
    heads = H // rep_total
    kv_heads = KVH // rep_total
    q_width = heads * HD
    kv_width = kv_heads * HD
    tok_count = block_input.shape[1]
    own_count = master.shape[1]
    tile_total = own_count * rep_total
    aligned = square() and whole_tiles(band_total, rep_total)
    tile_order = assignment[0]

    residual = block_input[0].astype(jnp.float32)
    grad_top = cotangent[0]
    position = band * tok_count + jnp.arange(tok_count, dtype=jnp.int32)
    cosine_table, sine_table = rope_tables(position)
    wide_cosine = jnp.concatenate([cosine_table, cosine_table], 1)[None]
    wide_sine = jnp.concatenate([sine_table, sine_table], 1)[None]
    scale_one = lax.rsqrt(jnp.mean(residual * residual, -1, keepdims=True) + norm_eps)
    normed_one = (residual * scale_one * gains[0]).astype(jnp.bfloat16)
    pick_rows = glob_select[0]
    glob_total = pick_rows.shape[0]
    selector = pick_rows.astype(jnp.bfloat16)
    glob_pos_part = jnp.sum(pick_rows * position[None, :], 1)
    digits = jnp.concatenate([glob_pos_part // 256, glob_pos_part % 256]).astype(jnp.bfloat16)
    digits = jnp.pad(digits[None], ((0, 7), (0, D - 2 * glob_total)))
    glob_rows = jnp.dot(selector, normed_one, preferred_element_type=jnp.float32).astype(jnp.bfloat16)
    glob_rows = add_all(jnp.concatenate([glob_rows, digits], 0), "fsdp").astype(jnp.bfloat16)
    packed = [normed_one, glob_rows, selector.reshape(-1, D)]
    packed = jnp.concatenate(packed, 0)
    packed = jnp.pad(packed, ((0, -packed.shape[0] % 32), (0, 0)))

    def over_bands(slice_rows):
        return lax.all_gather(slice_rows, "fsdp", axis=0, tiled=True)

    if aligned:
        half = BLK // 2
        low, high = (master[0, :, rows].astype(jnp.bfloat16) for rows in (slice(0, half), slice(half, BLK)))
        layout = slice_layout(band_total, rep_total)
        attn_layout = jnp.asarray(np.concatenate(layout[:4], 2))
        wanted = jnp.take(tile_order, by_place(attn_layout).reshape(-1), mode="clip")
        meta = jnp.stack([wanted // own_count == place, wanted % own_count], 0).astype(jnp.int32)
        attn_part = place_tiles(low, high, meta, *attn_layout.shape)
        attn_part = rep_scatter(attn_part).astype(jnp.bfloat16)
        low, attn_part = lax.optimization_barrier((low, attn_part))
        slots = square_pieces(low)
        attn = over_bands(attn_part)
        grids = [lax.dynamic_index_in_dim(jnp.asarray(grid), place, 0, False) for grid in layout]

        def find(wanted):
            wanted = jnp.take(tile_order, jnp.concatenate([grid.reshape(-1) for grid in wanted]), mode="clip")
            entry, row = (wanted // own_count) ^ place, wanted % own_count
            cut = own_count // 2
            high = (entry == 3) & (row >= cut)
            found = jnp.stack([jnp.where(high, 4, entry), jnp.where(high, row - cut, row)], 0)
            return found.astype(jnp.int32)

        all_grid = jnp.concatenate(grids[4:], 1)
        (first_part,) = gather_strips(slots, find([all_grid]), [all_grid.shape])
        packed, first_part, attn = lax.optimization_barrier((packed, first_part, attn))
        early = over_bands(first_part)
    packed_all = rep_gather(packed)
    if aligned:
        packed_all, high = lax.optimization_barrier((packed_all, high))
        later_slots = square_pieces(high)
    normed_one_all = packed_all[:, :tok_count].reshape(-1, D)
    at = tok_count + glob_total
    glob_digits = packed_all[:, at, : 2 * glob_total].astype(jnp.float32)
    glob_place = glob_digits[:, :glob_total] * 256.0 + glob_digits[:, glob_total:]
    at += 8
    selector_all = packed_all[:, at : at + selector.size // D].reshape(rep_total, glob_total, tok_count)

    if aligned:
        in_width = q_width + 2 * kv_width
        w_inner, w_output = attn[:, :in_width], attn[:, in_width:]
    else:
        slots = lax.all_gather(master[0].astype(jnp.bfloat16), "rep", axis=0, tiled=True)
        tiles = jnp.take(slots, tile_order, axis=0, mode="clip")
        slices = cut_slices(band_matrices(tiles, band_total), band_total, rep_total)
        w_inner = over_bands(jnp.concatenate(slices[0:3], 1))
        w_output = over_bands(slices[3])
        w_gate = over_bands(slices[4])
        w_up = over_bands(slices[5])
        w_down = over_bands(slices[6])

    w_output = by_place(w_output.reshape(rep_total, q_width, -1)).reshape(D, -1)

    def mul(rows, weight):
        return jnp.dot(rows, weight, preferred_element_type=jnp.float32)

    def mul_back(rows, weight):
        return lax.dot_general(rows, weight, (((1,), (1,)), ((), ())), preferred_element_type=jnp.float32)

    def weight_grad(rows, grad_rows):
        return lax.dot_general(
            rows, grad_rows, (((0,), (0,)), ((), ())), preferred_element_type=jnp.float32
        ).astype(jnp.bfloat16)

    def own_sum(partial):
        return rep_scatter(partial.astype(jnp.bfloat16).reshape(rep_total, tok_count, D))

    inner_rows = mul(packed_all.reshape(-1, D), w_inner).reshape(rep_total, -1, w_inner.shape[1])
    packed_all, normed_one_all = lax.optimization_barrier((packed_all, normed_one_all))
    queries, own_pairs = rope_rows(inner_rows, tok_count, 0, q_width, kv_width, wide_cosine, wide_sine)
    glob_cosine, glob_sine = rope_tables(glob_place.reshape(-1))
    glob_cosine = jnp.concatenate([glob_cosine, glob_cosine], 1).reshape(rep_total, glob_total, -1)
    glob_sine = jnp.concatenate([glob_sine, glob_sine], 1).reshape(rep_total, glob_total, -1)
    (glob_pairs,) = rope_rows(
        inner_rows, glob_total, tok_count // glob_total, q_width, kv_width, glob_cosine, glob_sine, False
    )
    back_count = (WINDOW + tok_count - 2) // tok_count
    odd = band % 2 == 1
    by_chip = back_count == 2 and band_total % 2 == 0
    if by_chip:
        two_back = shifted(own_pairs, "fsdp", 2)
        pair_blocks = [two_back, to_core(jnp.where(odd, two_back, own_pairs))]
    else:
        pair_blocks = [shifted(own_pairs, "fsdp", distance) for distance in range(back_count, 0, -1)]
    pair_blocks = pair_blocks + [own_pairs, glob_pairs]
    glob_spots = jnp.broadcast_to(glob_place[:, :, None], (rep_total, glob_total, BLK))
    band_number = band.astype(jnp.int32).reshape(1)
    attended_low, lse = attend(band_number, glob_spots, queries, pair_blocks)
    if aligned:
        *later_slots, attended_low, early = lax.optimization_barrier((*later_slots, attended_low, early))
        last_grid = jnp.concatenate(grids[4:6], 1)
        last_part, down_part = gather_strips(
            later_slots, find([last_grid, grids[6]]), [last_grid.shape, grids[6].shape]
        )

        def by_strips(gathered):
            return gathered.reshape(band_total, -1, all_grid.shape[0], half, gathered.shape[-1])

        early, late, late_down = by_strips(early), by_strips(over_bands(last_part)), by_strips(over_bands(down_part))
    attended_all = rep_features(attended_low).reshape(-1, D)
    columns = mul(attended_all, w_output).astype(jnp.bfloat16).reshape(rep_total, tok_count, -1)
    branch = by_place(rep_exchange(columns)).transpose(1, 0, 2).reshape(tok_count, D)
    middle = residual + branch.astype(jnp.float32)
    scale_two = lax.rsqrt(jnp.mean(middle * middle, -1, keepdims=True) + norm_eps)
    normed_two = (middle * scale_two * gains[1]).astype(jnp.bfloat16)
    normed_two_all = rep_gather(normed_two).reshape(-1, D)
    normed_two_all, grad_top_now = lax.optimization_barrier((normed_two_all, grad_top))
    top_first = gather_first(grad_top_now)

    if aligned:
        gate_rows, up_rows, activation = forward_products(normed_two_all, early, late, FF // rep_total)
        top_first, activation = after(top_first, activation)
        grad_top_all = gather_join(gather_second(top_first)).reshape(-1, D)
        g_down = weight_grad(activation, grad_top_all)
        grad_top_all, g_down = lax.optimization_barrier((grad_top_all, g_down))
        grad_gate, grad_up, pieces, branch_pieces = backward_products(
            grad_top_all, gate_rows, up_rows, activation, early, late, late_down
        )
        normed_first = sum_first(pieces)
        normed_first, g_gate = after(normed_first, weight_grad(normed_two_all, grad_gate))
        grad_normed_two = sum_second(normed_first)
    else:
        gate_rows = mul(normed_two_all, w_gate)
        up_rows = mul(normed_two_all, w_up)
        sigmoid_gate = jax.nn.sigmoid(gate_rows)
        silu_gate = gate_rows * sigmoid_gate
        activation = (silu_gate * up_rows).astype(jnp.bfloat16)
        grad_top_all = gather_join(gather_second(top_first)).reshape(-1, D)
        g_down = weight_grad(activation, grad_top_all)
        grad_act = mul_back(grad_top_all, w_down)
        grad_gate = (
            grad_act * up_rows * sigmoid_gate * (1.0 + gate_rows * (1.0 - sigmoid_gate))
        ).astype(jnp.bfloat16)
        grad_up = (grad_act * silu_gate).astype(jnp.bfloat16)
        grad_normed_two = own_sum(mul_back(grad_gate, w_gate) + mul_back(grad_up, w_up))
        branch_pieces = (mul(activation, w_down),)
        g_gate = weight_grad(normed_two_all, grad_gate)
    grad_normed_two, g_gate = lax.optimization_barrier((grad_normed_two, g_gate))

    def over_tokens(partial):
        return lax.psum_scatter(partial, "fsdp", scatter_dimension=0, tiled=True)

    s_down = over_tokens(g_down)
    s_gate = over_tokens(g_gate)

    grad_middle = grad_top.astype(jnp.float32) + norm_back(middle, scale_two, gains[1], grad_normed_two)
    grad_parts = grad_middle.astype(jnp.bfloat16).reshape(tok_count, rep_total, -1).transpose(1, 0, 2)
    grad_columns = rep_exchange(by_place(grad_parts)).reshape(rep_total * tok_count, -1)
    grad_columns, grad_up = lax.optimization_barrier((grad_columns, grad_up))
    grad_attended, g_up = rep_features_sum(
        grad_columns.reshape(rep_total, tok_count, -1),
        w_output,
        lambda: weight_grad(normed_two_all, grad_up),
    )
    grad_attended = grad_attended.astype(jnp.bfloat16)
    (s_down, g_up), grad_attended = after((s_down, g_up), grad_attended)
    down_first = gather_first(s_down)
    grad_queries, *grad_blocks = attend_back(
        band_number, glob_spots, wide_cosine, wide_sine, queries, grad_attended, lse, pair_blocks
    )
    down_first, *grad_blocks = after(down_first, *grad_blocks)
    down_second = gather_second(down_first)
    branch_pieces, *down_second = after(tuple(branch_pieces), *down_second)
    branch_first = sum_first(branch_pieces) if aligned else (own_sum(branch_pieces[0]),)
    if by_chip:
        came = to_core(jnp.concatenate([grad_blocks[1], grad_blocks[-1]], 1))
        came, glob_came = came[:, :tok_count], came[:, tok_count:]
        total = grad_blocks[0].astype(jnp.float32) + came.astype(jnp.float32)
        sent = jnp.where(odd, total.astype(jnp.bfloat16), grad_blocks[0])
        returned = [shifted(sent, "fsdp", -2), jnp.where(odd, jnp.zeros_like(came), came)]
    else:
        returned = [
            shifted(grad_blocks[back_count - distance], "fsdp", -distance)
            for distance in range(1, back_count + 1)
        ]
    if by_chip:
        glob_both = grad_blocks[-1].astype(jnp.float32) + glob_came.astype(jnp.float32)
        glob_grads = add_all(glob_both.astype(jnp.bfloat16), "fsdp", 2)
    else:
        glob_grads = add_all(grad_blocks[-1], "fsdp")
    branch_first, g_up, glob_grads, s_gate, *returned = lax.optimization_barrier(
        (branch_first, g_up, glob_grads, s_gate, *returned)
    )
    s_up = over_tokens(g_up)
    s_down = gather_join(down_second)
    gate_first = gather_first(s_gate)
    block_out = middle + (sum_second(branch_first) if aligned else branch_first[0])
    grad_inner = join_grads(
        grad_queries, grad_blocks[-2], selector_all, glob_grads, wide_cosine, wide_sine, returned
    ).reshape(-1, q_width + 2 * kv_width)
    grad_normed_parts = mul_back(grad_inner, w_inner).astype(jnp.bfloat16).reshape(rep_total, tok_count, D)
    if square():
        normed_first = sum_first(split_pieces(grad_normed_parts))
    else:
        normed_first = (rep_scatter(grad_normed_parts),)
    grad_inner, grad_normed_parts = lax.optimization_barrier((grad_inner, grad_normed_parts))
    g_inner = weight_grad(normed_one_all, grad_inner)
    attended_all, g_inner = lax.optimization_barrier((attended_all, g_inner))
    g_output = weight_grad(attended_all, grad_columns)
    g_output = by_place(g_output.reshape(rep_total, q_width, -1)).reshape(D, -1)
    g_attn = with_layout_constraint(jnp.concatenate([g_inner, g_output], 1), Layout((0, 1)))
    gate_first, block_out, *normed_first = after(gate_first, block_out, *normed_first)
    gate_second = gather_second(gate_first)
    grad_normed_one = sum_second(normed_first) if square() else normed_first[0]
    gate_second, s_up, g_attn, grad_normed_one = after(gate_second, s_up, g_attn, grad_normed_one)
    s_attn = over_tokens(g_attn)
    s_gate = gather_join(gate_second)
    up_first = gather_first(s_up)
    grad_input = grad_middle + norm_back(residual, scale_one, gains[0], grad_normed_one)

    gain_terms = jnp.stack(
        [
            jnp.sum(grad_normed_one * residual * scale_one, 0),
            jnp.sum(grad_normed_two * middle * scale_two, 0),
        ]
    )
    square_terms = jnp.stack(
        [jnp.sum(residual * residual), jnp.sum(middle * middle), jnp.sum(block_out * block_out)]
    )
    sums = jnp.concatenate([gain_terms.reshape(-1), square_terms])

    up_first, sums = after(up_first, sums)
    s_up = gather_join(gather_second(up_first))
    sums = add_all(add_all(sums, "rep"), "fsdp")
    sums, s_attn, s_up, s_gate, s_down = lax.optimization_barrier((sums, s_attn, s_up, s_gate, s_down))
    gain_grad, square_total = sums[: 2 * D].reshape(2, D), sums[2 * D :]

    slot_ids = jnp.arange(tile_total, dtype=jnp.int32)
    inverse = jnp.sum(jnp.where(tile_order[None, :] == slot_ids[:, None], slot_ids[None, :], 0), 1)
    own_slots = place * own_count + jnp.arange(own_count, dtype=jnp.int32)
    owned_tiles = jnp.take(inverse, own_slots, mode="clip")
    if aligned:
        sources = [rep_gather(s_attn), s_gate, s_up, s_down]
        where = np.zeros((4, rep_total, tile_total), np.int32)
        first_col = 0
        for kind, grid in enumerate(layout):
            rows, cols = grid.shape[1:]
            first_col = 0 if kind >= 4 else first_col
            for there in range(rep_total):
                numbers = grid[there].reshape(-1)
                at = np.arange(rows * cols)
                where[0, :, numbers] = max(kind - 3, 0)
                where[2, :, numbers] = (at // cols * BLK)[:, None]
                where[3, :, numbers] = (at % cols * BLK + first_col)[:, None]
                for here in range(rep_total):
                    where[1, here, numbers] = here ^ there
            first_col += cols * BLK
        tile_spots = lax.dynamic_index_in_dim(jnp.asarray(where), place, 1, False)
        meta = jnp.take(tile_spots, owned_tiles, axis=1, mode="clip")
    else:
        splits = [0, q_width, q_width + kv_width, q_width + 2 * kv_width, s_attn.shape[1]]
        stacks = [rep_gather(s_attn[:, low:high]) for low, high in zip(splits, splits[1:])]
        stacks += [s_gate, s_up, s_down]
        sources = [band_tiles(join_slices(stacks, band_total, rep_total))]
        meta = jnp.stack([0 * owned_tiles, owned_tiles, 0 * owned_tiles, 0 * owned_tiles], 0)
    slot_rates = jnp.take(kind_rates(band_total), owned_tiles, mode="clip")
    new_first, new_second, new_master, master_copy = adam(
        meta,
        slot_rates,
        (master[0], first_moment[0], second_moment[0], left_basis[0], right_basis[0]),
        sources,
    )
    new_gain_first = beta_one * gain_first + (1.0 - beta_one) * gain_grad
    new_gain_second = beta_two * gain_second + (1.0 - beta_two) * gain_grad * gain_grad
    gain_step = (
        new_gain_first
        / (1.0 - beta_one**STEP)
        / (jnp.sqrt(new_gain_second / (1.0 - beta_two**STEP)) + adam_eps)
    )
    new_gains = gains - gain_rate * gain_step
    rms_stats = jnp.sqrt(square_total / (rep_total * band_total * tok_count * D))
    return (
        block_out[None],
        grad_input[None],
        new_first[None],
        new_second[None],
        new_master[None],
        master_copy[None],
        new_gain_first,
        new_gain_second,
        new_gains,
        rms_stats,
    )


def solution(mesh):
    in_specs = (
        P("rep", "fsdp", None),
        P("rep", "fsdp", None),
        P("rep", None, "fsdp"),
        P("fsdp", None),
        P("fsdp", "rep", None, None),
        P("fsdp", "rep", None, None),
        P("fsdp", "rep", None, None),
        P("fsdp", "rep", None, None),
        P("fsdp", "rep", None, None),
        P(),
        P(),
        P(),
    )
    out_specs = (
        P("rep", "fsdp", None),
        P("rep", "fsdp", None),
        P("fsdp", "rep", None, None),
        P("fsdp", "rep", None, None),
        P("fsdp", "rep", None, None),
        P("fsdp", "rep", None, None),
        P(),
        P(),
        P(),
        P(),
    )
    return jax.shard_map(
        per_device, mesh=mesh, in_specs=in_specs, out_specs=out_specs, check_vma=False
    )
```

profile of v0, /device:TPU:0, one launch (start us, length us, event | category | flops | bytes accessed | tf_op | source)
XLA Modules:
  0.0 869.7 jit_solution(17669669168209999967)
XLA Ops:
  10.4 4.0 convert.30
  23.6 12.9 %collective-permute-done.4 = bf16[2,256,640]{2,1,0:T(8,128)(2,1)S(1)} collective-permute-done((bf16[2,256,640]{2,1,0:T(8,128)(2,1)S(1)}, bf16[2,256,640]{2,1,0:T(8,128)(2,1)S(1)}, u32[]{:S(2)}, u32[]{:S(2)}) %collective-permute-start.4) | collective-permute-done | bytes 655392 | tf_op jit(solution)/shard_map/ppermute | solution.py:107
  40.8 5.7 collective-permute-done.5
  76.3 16.3 %collective-permute-done.9.refs_2_ = bf16[116,64,128]{2,1,0:T(8,128)(2,1)} collective-permute-done((bf16[116,64,128]{2,1,0:T(8,128)(2,1)S(1)}, bf16[116,64,128]{2,1,0:T(8,128)(2,1)}, u32[]{:S(2)}, u32[]{:S(2)}) %collective-permute-start.9) | collective-permute-done | bytes 1900576 | tf_op jit(solution)/shard_map/ppermute | solution.py:107
  99.7 27.8 %collective-permute-done.2 = bf16[72,2048]{1,0:T(8,128)(2,1)} collective-permute-done((bf16[72,2048]{1,0:T(8,128)(2,1)}, bf16[72,2048]{1,0:T(8,128)(2,1)}, u32[]{:S(2)}, u32[]{:S(2)}) %collective-permute-start.2) | collective-permute-done | bytes 294944 | tf_op jit(solution)/shard_map/ppermute | solution.py:196
  131.4 5.8 shard_map.241
  142.5 28.7 %collective-permute-done.12 = bf16[352,2048]{1,0:T(8,128)(2,1)S(1)} collective-permute-done((bf16[352,2048]{1,0:T(8,128)(2,1)}, bf16[352,2048]{1,0:T(8,128)(2,1)S(1)}, u32[]{:S(2)}, u32[]{:S(2)}) %collective-permute-start.12) | collective-permute-done | bytes 1441824 | tf_op jit(solution)/shard_map/ppermute | solution.py:107
  174.5 14.2 %collective-permute-done.14 = bf16[176,2048]{1,0:T(8,128)(2,1)S(1)} collective-permute-done((bf16[176,2048]{1,0:T(8,128)(2,1)S(1)}, bf16[176,2048]{1,0:T(8,128)(2,1)S(1)}, u32[]{:S(2)}, u32[]{:S(2)}) %collective-permute-start.14) | collective-permute-done | bytes 720928 | tf_op jit(solution)/shard_map/ppermute | solution.py:107
  192.7 6.1 fusion.x_ref
  198.8 4.6 shard_map.242
  206.0 21.7 %collective-permute-done.20.refs_0_ = bf16[4,256,256]{2,1,0:T(8,128)(2,1)S(1)} collective-permute-done((bf16[4,256,256]{2,1,0:T(8,128)(2,1)}, bf16[4,256,256]{2,1,0:T(8,128)(2,1)S(1)}, u32[]{:S(2)}, u32[]{:S(2)}) %collective-permute-start.20) | collective-permute-done | bytes 524320 | tf_op jit(solution)/shard_map/ppermute | solution.py:280
  249.3 17.0 %shard_map.244 = (bf16[4,256,512]{2,1,0:T(8,128)(2,1)S(1)}, f32[4,8,256]{2,1,0:T(8,128)S(1)}) custom-call(s32[1]{0:T(128)} %bitcast.25.band_ref, f32[4,64,128]{2,1,0:T(8,128)S(1)} %broadcast_in_dim.83.gpos_ref, bf16[4,256,512]{2,1,0:T(8,128)(2,1)S(1)} %copy-done.18, bf16[4,256,256]{2,1,0:T(8,128)(2,1)S(1)} %copy-done.13, ...), custom_call_target="tpu_custom_call" | custom-call | flops 6979321856 | bytes 2097152 | tf_op jit(solution)/shard_map/pallas_call | solution.py:747
  266.4 5.4 shard_map.245
  273.7 21.6 %collective-permute-done.23 = bf16[4,256,512]{2,1,0:T(8,128)(2,1)S(1)} collective-permute-done((bf16[4,256,512]{2,1,0:T(8,128)(2,1)S(1)}, bf16[4,256,512]{2,1,0:T(8,128)(2,1)S(1)}, u32[]{:S(2)}, u32[]{:S(2)}) %collective-permute-start.23) | collective-permute-done | bytes 1048608 | tf_op jit(solution)/shard_map/ppermute | solution.py:107
  297.9 9.3 %collective-permute-done.24 = bf16[2,256,512]{2,1,0:T(8,128)(2,1)S(1)} collective-permute-done((bf16[2,256,512]{2,1,0:T(8,128)(2,1)S(1)}, bf16[2,256,512]{2,1,0:T(8,128)(2,1)S(1)}, u32[]{:S(2)}, u32[]{:S(2)}) %collective-permute-start.24) | collective-permute-done | bytes 524320 | tf_op jit(solution)/shard_map/ppermute | solution.py:107
  315.0 5.5 collective-permute-done.28
  334.5 21.5 %collective-permute-done.29 = bf16[256,2048]{1,0:T(8,128)(2,1)S(1)} collective-permute-done((bf16[256,2048]{1,0:T(8,128)(2,1)S(1)}, bf16[256,2048]{1,0:T(8,128)(2,1)S(1)}, u32[]{:S(2)}, u32[]{:S(2)}) %collective-permute-start.29) | collective-permute-done | bytes 1048608 | tf_op jit(solution)/shard_map/ppermute | solution.py:107
  360.3 8.1 collective-permute-done.31
  372.0 24.7 %shard_map.246 = (bf16[1024,2048]{1,0:T(8,128)(2,1)S(1)}, bf16[1024,2048]{1,0:T(8,128)(2,1)}, bf16[1024,2048]{1,0:T(8,128)(2,1)}) custom-call(bf16[1024,2048]{1,0:T(8,128)(2,1)} %constant_dynamic-update-slice_fusion.5.x_ref, bf16[8,24,2,64,256]{4,3,2,1,0:T(8,128)(2,1)} %bitcast.288, bf16[8,16,2,64,256]{4,3,2,1,0:T(8,128)(2,1)} %bitcast.290), custom_call_target="tpu_custom_call" | custom-call | flops 536870912 | bytes 4194304 | tf_op jit(solution)/shard_map/pallas_call | solution.py:518
  404.7 5.8 collective-permute-done.35
  412.6 11.4 %convolution_convert_fusion.2 = bf16[2048,2048]{1,0:T(8,128)(2,1)} fusion(bf16[1024,2048]{1,0:T(8,128)(2,1)S(1)} %copy-done.79, bf16[1024,2048]{1,0:T(8,128)(2,1)S(1)} %constant_dynamic-update-slice_fusion.10.top_ref), kind=kOutput, calls=%fused_computation.8 | convolution fusion | flops 8594128896 | bytes 16777216 | tf_op jit(solution)/shard_map/dot_general | solution.py:1093
  424.3 48.1 %shard_map.247 = (bf16[1024,2048]{1,0:T(8,128)(2,1)}, bf16[1024,2048]{1,0:T(8,128)(2,1)}, bf16[2,256,1024]{2,1,0:T(8,128)(2,1)}, bf16[2,256,1024]{2,1,0:T(8,128)...) custom-call(bf16[1024,2048]{1,0:T(8,128)(2,1)} %copy-done.60, ...), custom_call_target="tpu_custom_call" | custom-call | flops 34359738368 | bytes 33554432 | tf_op jit(solution)/shard_map/pallas_call | solution.py:615
  474.6 14.4 %convolution_convert_fusion.1 = bf16[2048,2048]{1,0:T(8,128)(2,1)} fusion(bf16[1024,2048]{1,0:T(8,128)(2,1)} %constant_dynamic-update-slice_fusion.5.x_ref, bf16[1024,2048]{1,0:T(8,128)(2,1)} %get-tuple-element.173), kind=kOutput, calls=%fused_computation.7 | convolution fusion | flops 8594128896 | bytes 16777216 | tf_op jit(solution)/shard_map/dot_general | solution.py:1093
  489.0 4.7 collective-permute-done.37
  499.3 7.2 collective-permute-done.39
  509.8 4.1 multiply_reduce_fusion.1
  524.0 3.8 collective-permute-done.43
  530.7 3.7 shard_map.248
  537.3 13.8 %convolution_convert_fusion = bf16[2048,2048]{1,0:T(8,128)(2,1)} fusion(bf16[1024,2048]{1,0:T(8,128)(2,1)} %constant_dynamic-update-slice_fusion.5.x_ref, bf16[1024,2048]{1,0:T(8,128)(2,1)S(1)} %copy-done.82), kind=kOutput, calls=%fused_computation.6 | convolution fusion | flops 8594128896 | bytes 16777216 | tf_op jit(solution)/shard_map/dot_general | solution.py:1093
  560.5 11.0 %collective-permute-done.46 = bf16[1024,256]{1,0:T(8,128)(2,1)S(1)} collective-permute-done((bf16[1024,256]{1,0:T(8,128)(2,1)S(1)}, bf16[1024,256]{1,0:T(8,128)(2,1)S(1)}, u32[]{:S(2)}, u32[]{:S(2)}) %collective-permute-start.46) | collective-permute-done | bytes 524320 | tf_op jit(solution)/shard_map/ppermute | solution.py:107
  576.4 25.9 %shard_map.249 = (bf16[4,256,512]{2,1,0:T(8,128)(2,1)S(1)}, bf16[4,256,256]{2,1,0:T(8,128)(2,1)S(1)}, bf16[4,256,256]{2,1,0:T(8,128)(2,1)S(1)}, f32[4,256,256]{2,1,0:T(8,128)S(1)}, bf16[4,64,256]{2,1,0:T(8,128)(2,1)S(1)}) custom-call(s32[1]{0:T(128)} %bitcast.25.band_ref, f32[4,64,128]{2,1,0:T(8,128)S(1)} %broadcast_in_dim.83.gpos_ref, ...), custom_call_target="tpu_custom_call" | custom-call | flops 17448304640 | bytes 4194304 | tf_op jit(solution)/shard_map/pallas_call | solution.py:833
  605.5 9.0 %collective-permute-done.51 = bf16[128,2048]{1,0:T(8,128)(2,1)S(1)} collective-permute-done((bf16[128,2048]{1,0:T(8,128)(2,1)S(1)}, bf16[128,2048]{1,0:T(8,128)(2,1)S(1)}, u32[]{:S(2)}, u32[]{:S(2)}) %collective-permute-start.51) | collective-permute-done | bytes 524320 | tf_op jit(solution)/shard_map/ppermute | solution.py:107
  619.8 18.8 %collective-permute-start.57 = (bf16[4,64,256]{2,1,0:T(8,128)(2,1)S(1)}, bf16[4,64,256]{2,1,0:T(8,128)(2,1)S(1)}, u32[]{:S(2)}, u32[]{:S(2)}) collective-permute-start(bf16[4,64,256]{2,1,0:T(8,128)(2,1)S(1)} %add_convert_fusion.14), channel_id=1, source_target_pairs={{0,6},{1,7},{2,4},{3,5},{4,2},{5,3},{6,0},{7,1},{8,14},{9,15},{10,... | collective-permute-start | bytes 393224 | tf_op jit(solution)/shard_map/ppermute | solution.py:196
  644.3 4.1 collective-permute-done.56
  651.5 3.8 collective-permute-done.58.refs_0_
  657.0 4.8 slice.407
  664.7 5.2 shard_map.250
  670.0 6.0 convolution_convert_fusion.3
  676.0 3.9 convolution_convert_fusion.4
  686.0 9.7 %collective-permute-done.61 = bf16[256,1024]{1,0:T(8,128)(2,1)S(1)} collective-permute-done((bf16[256,1024]{1,0:T(8,128)(2,1)S(1)}, bf16[256,1024]{1,0:T(8,128)(2,1)S(1)}, u32[]{:S(2)}, u32[]{:S(2)}) %collective-permute-start.61) | collective-permute-done | bytes 524320 | tf_op jit(solution)/shard_map/ppermute | solution.py:107
  700.6 14.4 %collective-permute-done.63 = bf16[2,256,1024]{2,1,0:T(8,128)(2,1)S(1)} collective-permute-done((bf16[2,256,1024]{2,1,0:T(8,128)(2,1)S(1)}, bf16[2,256,1024]{2,1,0:T(8,128)(2,1)S(1)}, u32[]{:S(2)}, u32[]{:S(2)}) %collective-permute-start.63) | collective-permute-done | bytes 1048608 | tf_op jit(solution)/shard_map/ppermute | solution.py:107
  730.9 4.3 collective-permute-done.66
  735.2 10.0 %reduce-scatter.9.cloned.1.call-done = bf16[256,2048]{1,0:T(8,128)(2,1)} async-done(((bf16[2048,2048]{1,0:T(8,128)(2,1)}), bf16[256,2048]{1,0:T(8,128)(2,1)}) %reduce-scatter.9.cloned.1.call-update) | async-done | bytes 1048592 | tf_op jit(solution)/shard_map/reduce_scatter | solution.py:1173
  775.1 4.1 collective-permute-done.70
  803.3 4.4 reduce-scatter.11.cloned.1.call-done
  813.1 9.3 %collective-permute-done.81 = bf16[256,1280]{1,0:T(8,128)(2,1)S(1)} collective-permute-done((bf16[256,1280]{1,0:T(8,128)(2,1)}, bf16[256,1280]{1,0:T(8,128)(2,1)S(1)}, u32[]{:S(2)}, u32[]{:S(2)}) %collective-permute-start.81) | collective-permute-done | bytes 655392 | tf_op jit(solution)/shard_map/ppermute | solution.py:107
  827.5 5.6 collective-permute-done.82
  834.6 27.7 %shard_map.251 = (f32[116,128,128]{2,1,0:T(8,128)}, f32[116,128,128]{2,1,0:T(8,128)}, f32[116,128,128]{2,1,0:T(8,128)}, bf16[116,128,128]{2,1,0:T(8,128)(2,1)}) custom-call(s32[4,116]{1,0:T(4,128)} %bitcast.338, f32[116]{0:T(128)} %gather_fusion.5, f32[116,128,128]{2,1,0:T(8,128)} %bitcast.287, f32[116,128,128]{2,1,0:T(8,128)} %bitcast.296, ...), custom_call_target="tpu_custom_call" | custom-call | flops 1946157056 | bytes 68419584 | tf_op jit(solution)/shard_map/pallas_call | solution.py:962
  (524 shorter events, 293.6 us)
Async XLA Ops:
  7.2 130.1 %all-gather.5.cloned.1.call-start = ((), (), s32[]{:S(2)}) async-start(), calls=%async_computation.4 | async-start | bytes 5898240 | tf_op jit(solution)/shard_map/all_gather | solution.py:1032
  19.0 17.6 %collective-permute-start.4 = (bf16[2,256,640]{2,1,0:T(8,128)(2,1)S(1)}, bf16[2,256,640]{2,1,0:T(8,128)(2,1)S(1)}, u32[]{:S(2)}, u32[]{:S(2)}) collective-permute-start(bf16[2,256,640]{2,1,0:T(8,128)(2,1)S(1)} %pad_maximum_fusion.9), channel_id=1, source_target_pairs={{0,8},{8,0},{16,24},{24,16},{1,9},{9,1},{17,25},{25,17},{2,10},{10... | collective-permute-start | bytes 1966088 | tf_op jit(solution)/shard_map/ppermute | solution.py:107
  48.9 217.4 %all-gather.7.cloned.1.call-start = ((), (), s32[]{:S(2)}) async-start(), calls=%async_computation.5 | async-start | bytes 14155776 | tf_op jit(solution)/shard_map/all_gather | solution.py:1032
  51.8 40.8 %collective-permute-start.9 = (bf16[116,64,128]{2,1,0:T(8,128)(2,1)S(1)}, bf16[116,64,128]{2,1,0:T(8,128)(2,1)}, u32[]{:S(2)}, u32[]{:S(2)}) collective-permute-start(bf16[116,64,128]{2,1,0:T(8,128)(2,1)S(1)} %get-tuple-element.135.low.refs_0_), channel_id=1, source_target_pairs={{0,16},{8,24},{16,0},{24,8},{1,17},{9,25},{17,1},{25,9},{2,18},{10... | collective-permute-start | bytes 5701640 | tf_op jit(solution)/shard_map/ppermute | solution.py:107
  52.4 44.2 %collective-permute-start.8 = (bf16[116,64,128]{2,1,0:T(8,128)(2,1)S(1)}, bf16[116,64,128]{2,1,0:T(8,128)(2,1)}, u32[]{:S(2)}, u32[]{:S(2)}) collective-permute-start(bf16[116,64,128]{2,1,0:T(8,128)(2,1)S(1)} %get-tuple-element.135.low.refs_0_), channel_id=1, source_target_pairs={{0,8},{8,0},{16,24},{24,16},{1,9},{9,1},{17,25},{25,17},{2,10},{10... | collective-permute-start | bytes 5701640 | tf_op jit(solution)/shard_map/ppermute | solution.py:107
  54.5 16.6 %collective-permute-start = (bf16[72,2048]{1,0:T(8,128)(2,1)}, bf16[72,2048]{1,0:T(8,128)(2,1)S(1)}, u32[]{:S(2)}, u32[]{:S(2)}) collective-permute-start(bf16[72,2048]{1,0:T(8,128)(2,1)} %pad_maximum_fusion.12), channel_id=1, source_target_pairs={{0,1},{1,0},{2,3},{3,2},{4,5},{5,4},{6,7},{7,6},{8,9},{9,8},{10,11... | collective-permute-start | bytes 884744 | tf_op jit(solution)/shard_map/ppermute | solution.py:196
  71.9 27.8 %collective-permute-start.3 = (bf16[72,2048]{1,0:T(8,128)(2,1)}, bf16[72,2048]{1,0:T(8,128)(2,1)}, u32[]{:S(2)}, u32[]{:S(2)}) collective-permute-start(bf16[72,2048]{1,0:T(8,128)(2,1)} %fusion.36), channel_id=1, source_target_pairs={{0,6},{1,7},{2,4},{3,5},{4,2},{5,3},{6,0},{7,1},{8,14},{9,15},{10,... | collective-permute-start | bytes 884744 | tf_op jit(solution)/shard_map/ppermute | solution.py:196
  74.9 52.6 %collective-permute-start.2 = (bf16[72,2048]{1,0:T(8,128)(2,1)}, bf16[72,2048]{1,0:T(8,128)(2,1)}, u32[]{:S(2)}, u32[]{:S(2)}) collective-permute-start(bf16[72,2048]{1,0:T(8,128)(2,1)} %fusion.36), channel_id=1, source_target_pairs={{0,4},{1,5},{2,6},{3,7},{4,0},{5,1},{6,2},{7,3},{8,12},{9,13},{10,... | collective-permute-start | bytes 884744 | tf_op jit(solution)/shard_map/ppermute | solution.py:196
  74.9 52.6 %collective-permute-start.1 = (bf16[72,2048]{1,0:T(8,128)(2,1)}, bf16[72,2048]{1,0:T(8,128)(2,1)}, u32[]{:S(2)}, u32[]{:S(2)}) collective-permute-start(bf16[72,2048]{1,0:T(8,128)(2,1)} %fusion.36), channel_id=1, source_target_pairs={{0,2},{1,3},{2,0},{3,1},{4,6},{5,7},{6,4},{7,5},{8,10},{9,11},{10,... | collective-permute-start | bytes 884744 | tf_op jit(solution)/shard_map/ppermute | solution.py:196
  94.8 36.6 %collective-permute-start.11 = (bf16[58,64,128]{2,1,0:T(8,128)(2,1)}, bf16[58,64,128]{2,1,0:T(8,128)(2,1)S(1)}, u32[]{:S(2)}, u32[]{:S(2)}) collective-permute-start(bf16[58,64,128]{2,1,0:T(8,128)(2,1)} %slice.440), channel_id=1, source_target_pairs={{0,8},{8,0},{16,24},{24,16},{1,9},{9,1},{17,25},{25,17},{2,10},{10... | collective-permute-start | bytes 2850824 | tf_op jit(solution)/shard_map/ppermute | solution.py:107
  98.7 32.7 %collective-permute-start.10 = (bf16[58,64,128]{2,1,0:T(8,128)(2,1)}, bf16[58,64,128]{2,1,0:T(8,128)(2,1)}, u32[]{:S(2)}, u32[]{:S(2)}) collective-permute-start(bf16[58,64,128]{2,1,0:T(8,128)(2,1)} %slice.439), channel_id=1, source_target_pairs={{0,16},{8,24},{16,0},{24,8},{1,17},{9,25},{17,1},{25,9},{2,18},{10... | collective-permute-start | bytes 2850824 | tf_op jit(solution)/shard_map/ppermute | solution.py:107
  137.3 234.7 %all-gather.9.cloned.1.call-start = ((), (), s32[]{:S(2)}) async-start(), calls=%async_computation.6 | async-start | bytes 9437184 | tf_op jit(solution)/shard_map/all_gather | solution.py:1032
  137.3 33.9 %collective-permute-start.12 = (bf16[352,2048]{1,0:T(8,128)(2,1)}, bf16[352,2048]{1,0:T(8,128)(2,1)S(1)}, u32[]{:S(2)}, u32[]{:S(2)}) collective-permute-start(bf16[352,2048]{1,0:T(8,128)(2,1)} %fusion.28), channel_id=1, source_target_pairs={{0,8},{8,0},{16,24},{24,16},{1,9},{9,1},{17,25},{25,17},{2,10},{10... | collective-permute-start | bytes 4325384 | tf_op jit(solution)/shard_map/ppermute | solution.py:107
  138.9 33.9 %collective-permute-start.13 = (bf16[352,2048]{1,0:T(8,128)(2,1)}, bf16[352,2048]{1,0:T(8,128)(2,1)S(1)}, u32[]{:S(2)}, u32[]{:S(2)}) collective-permute-start(bf16[352,2048]{1,0:T(8,128)(2,1)} %fusion.28), channel_id=1, source_target_pairs={{0,16},{8,24},{16,0},{24,8},{1,17},{9,25},{17,1},{25,9},{2,18},{10... | collective-permute-start | bytes 4325384 | tf_op jit(solution)/shard_map/ppermute | solution.py:107
  171.3 17.5 %collective-permute-start.14 = (bf16[176,2048]{1,0:T(8,128)(2,1)S(1)}, bf16[176,2048]{1,0:T(8,128)(2,1)S(1)}, u32[]{:S(2)}, u32[]{:S(2)}) collective-permute-start(bf16[176,2048]{1,0:T(8,128)(2,1)S(1)} %slice.441), channel_id=1, source_target_pairs={{0,16},{8,24},{16,0},{24,8},{1,17},{9,25},{17,1},{25,9},{2,18},{10... | collective-permute-start | bytes 2162696 | tf_op jit(solution)/shard_map/ppermute | solution.py:107
  172.9 17.2 %collective-permute-start.15 = (bf16[176,2048]{1,0:T(8,128)(2,1)S(1)}, bf16[176,2048]{1,0:T(8,128)(2,1)S(1)}, u32[]{:S(2)}, u32[]{:S(2)}) collective-permute-start(bf16[176,2048]{1,0:T(8,128)(2,1)S(1)} %slice.442), channel_id=1, source_target_pairs={{0,8},{8,0},{16,24},{24,16},{1,9},{9,1},{17,25},{25,17},{2,10},{10... | collective-permute-start | bytes 2162696 | tf_op jit(solution)/shard_map/ppermute | solution.py:107
  190.1 41.8 %collective-permute-start.17 = (bf16[116,64,128]{2,1,0:T(8,128)(2,1)S(1)}, bf16[116,64,128]{2,1,0:T(8,128)(2,1)}, u32[]{:S(2)}, u32[]{:S(2)}) collective-permute-start(bf16[116,64,128]{2,1,0:T(8,128)(2,1)S(1)} %copy-done.1), channel_id=1, source_target_pairs={{0,16},{8,24},{16,0},{24,8},{1,17},{9,25},{17,1},{25,9},{2,18},{10... | collective-permute-start | bytes 5701640 | tf_op jit(solution)/shard_map/ppermute | solution.py:107
  190.9 44.1 %collective-permute-start.16 = (bf16[116,64,128]{2,1,0:T(8,128)(2,1)S(1)}, bf16[116,64,128]{2,1,0:T(8,128)(2,1)}, u32[]{:S(2)}, u32[]{:S(2)}) collective-permute-start(bf16[116,64,128]{2,1,0:T(8,128)(2,1)S(1)} %copy-done.1), channel_id=1, source_target_pairs={{0,8},{8,0},{16,24},{24,16},{1,9},{9,1},{17,25},{25,17},{2,10},{10... | collective-permute-start | bytes 5701640 | tf_op jit(solution)/shard_map/ppermute | solution.py:107
  203.4 24.3 %collective-permute-start.20 = (bf16[4,256,256]{2,1,0:T(8,128)(2,1)}, bf16[4,256,256]{2,1,0:T(8,128)(2,1)S(1)}, u32[]{:S(2)}, u32[]{:S(2)}) collective-permute-start(bf16[4,256,256]{2,1,0:T(8,128)(2,1)} %get-tuple-element.142.refs_2_), channel_id=1, source_target_pairs={{0,2},{1,3},{2,4},{3,5},{4,6},{5,7},{8,10},{9,11},{10,12},{11,13},... | collective-permute-start | bytes 1572872 | tf_op jit(solution)/shard_map/ppermute | solution.py:280
  234.1 32.2 %collective-permute-start.19 = (bf16[58,64,128]{2,1,0:T(8,128)(2,1)}, bf16[58,64,128]{2,1,0:T(8,128)(2,1)}, u32[]{:S(2)}, u32[]{:S(2)}) collective-permute-start(bf16[58,64,128]{2,1,0:T(8,128)(2,1)} %slice.444), channel_id=1, source_target_pairs={{0,8},{8,0},{16,24},{24,16},{1,9},{9,1},{17,25},{25,17},{2,10},{10... | collective-permute-start | bytes 2850824 | tf_op jit(solution)/shard_map/ppermute | solution.py:107
  237.2 29.1 %collective-permute-start.18 = (bf16[58,64,128]{2,1,0:T(8,128)(2,1)}, bf16[58,64,128]{2,1,0:T(8,128)(2,1)}, u32[]{:S(2)}, u32[]{:S(2)}) collective-permute-start(bf16[58,64,128]{2,1,0:T(8,128)(2,1)} %slice.443), channel_id=1, source_target_pairs={{0,16},{8,24},{16,0},{24,8},{1,17},{9,25},{17,1},{25,9},{2,18},{10... | collective-permute-start | bytes 2850824 | tf_op jit(solution)/shard_map/ppermute | solution.py:107
  271.8 152.5 %all-gather.11.cloned.1.call-start = ((), (), s32[]{:S(2)}) async-start(), calls=%async_computation.7 | async-start | bytes 4718592 | tf_op jit(solution)/shard_map/all_gather | solution.py:1032
  271.8 23.5 %collective-permute-start.23 = (bf16[4,256,512]{2,1,0:T(8,128)(2,1)S(1)}, bf16[4,256,512]{2,1,0:T(8,128)(2,1)S(1)}, u32[]{:S(2)}, u32[]{:S(2)}) collective-permute-start(bf16[4,256,512]{2,1,0:T(8,128)(2,1)S(1)} %get-tuple-element.145), channel_id=1, source_target_pairs={{0,16},{8,24},{16,0},{24,8},{1,17},{9,25},{17,1},{25,9},{2,18},{10... | collective-permute-start | bytes 3145736 | tf_op jit(solution)/shard_map/ppermute | solution.py:107
  272.6 23.8 %collective-permute-start.22 = (bf16[4,256,512]{2,1,0:T(8,128)(2,1)S(1)}, bf16[4,256,512]{2,1,0:T(8,128)(2,1)S(1)}, u32[]{:S(2)}, u32[]{:S(2)}) collective-permute-start(bf16[4,256,512]{2,1,0:T(8,128)(2,1)S(1)} %get-tuple-element.145), channel_id=1, source_target_pairs={{0,8},{8,0},{16,24},{24,16},{1,9},{9,1},{17,25},{25,17},{2,10},{10... | collective-permute-start | bytes 3145736 | tf_op jit(solution)/shard_map/ppermute | solution.py:107
  314.8 260.4 %reduce-scatter.5.cloned.1.call-start = ((), (), s32[]{:S(2)}) async-start(), calls=%async_computation.8 | async-start | bytes 9437184 | tf_op jit(solution)/shard_map/reduce_scatter | solution.py:1173
  332.4 23.5 %collective-permute-start.29 = (bf16[256,2048]{1,0:T(8,128)(2,1)S(1)}, bf16[256,2048]{1,0:T(8,128)(2,1)S(1)}, u32[]{:S(2)}, u32[]{:S(2)}) collective-permute-start(bf16[256,2048]{1,0:T(8,128)(2,1)S(1)} %get-tuple-element.272), channel_id=1, source_target_pairs={{0,8},{8,0},{16,24},{24,16},{1,9},{9,1},{17,25},{25,17},{2,10},{10... | collective-permute-start | bytes 3145736 | tf_op jit(solution)/shard_map/ppermute | solution.py:107
  333.8 24.4 %collective-permute-start.30 = (bf16[256,2048]{1,0:T(8,128)(2,1)S(1)}, bf16[256,2048]{1,0:T(8,128)(2,1)S(1)}, u32[]{:S(2)}, u32[]{:S(2)}) collective-permute-start(bf16[256,2048]{1,0:T(8,128)(2,1)S(1)} %get-tuple-element.272), channel_id=1, source_target_pairs={{0,16},{8,24},{16,0},{24,8},{1,17},{9,25},{17,1},{25,9},{2,18},{10... | collective-permute-start | bytes 3145736 | tf_op jit(solution)/shard_map/ppermute | solution.py:107
  370.1 26.6 %collective-permute-start.34 = (bf16[256,2048]{1,0:T(8,128)(2,1)S(1)}, bf16[256,2048]{1,0:T(8,128)(2,1)}, u32[]{:S(2)}, u32[]{:S(2)}) collective-permute-start(bf16[256,2048]{1,0:T(8,128)(2,1)S(1)} %bitcast.311), channel_id=1, source_target_pairs={{0,16},{8,24},{16,0},{24,8},{1,17},{9,25},{17,1},{25,9},{2,18},{10... | collective-permute-start | bytes 3145736 | tf_op jit(solution)/shard_map/ppermute | solution.py:107
  370.8 25.9 %collective-permute-start.33 = (bf16[256,2048]{1,0:T(8,128)(2,1)S(1)}, bf16[256,2048]{1,0:T(8,128)(2,1)}, u32[]{:S(2)}, u32[]{:S(2)}) collective-permute-start(bf16[256,2048]{1,0:T(8,128)(2,1)S(1)} %bitcast.312), channel_id=1, source_target_pairs={{0,8},{8,0},{16,24},{24,16},{1,9},{9,1},{17,25},{25,17},{2,10},{10... | collective-permute-start | bytes 3145736 | tf_op jit(solution)/shard_map/ppermute | solution.py:107
  424.0 227.5 %reduce-scatter.7.cloned.1.call-start = ((), (), s32[]{:S(2)}) async-start(), calls=%async_computation.9 | async-start | bytes 9437184 | tf_op jit(solution)/shard_map/reduce_scatter | solution.py:1173
  472.4 21.2 %collective-permute-start.37 = (bf16[2,256,1024]{2,1,0:T(8,128)(2,1)}, bf16[2,256,1024]{2,1,0:T(8,128)(2,1)}, u32[]{:S(2)}, u32[]{:S(2)}) collective-permute-start(bf16[2,256,1024]{2,1,0:T(8,128)(2,1)} %get-tuple-element.170), channel_id=1, source_target_pairs={{0,8},{8,0},{16,24},{24,16},{1,9},{9,1},{17,25},{25,17},{2,10},{10... | collective-permute-start | bytes 3145736 | tf_op jit(solution)/shard_map/ppermute | solution.py:107
  474.0 21.6 %collective-permute-start.38 = (bf16[2,256,1024]{2,1,0:T(8,128)(2,1)}, bf16[2,256,1024]{2,1,0:T(8,128)(2,1)}, u32[]{:S(2)}, u32[]{:S(2)}) collective-permute-start(bf16[2,256,1024]{2,1,0:T(8,128)(2,1)} %get-tuple-element.172), channel_id=1, source_target_pairs={{0,16},{8,24},{16,0},{24,8},{1,17},{9,25},{17,1},{25,9},{2,18},{10... | collective-permute-start | bytes 3145736 | tf_op jit(solution)/shard_map/ppermute | solution.py:107
  509.7 235.5 %reduce-scatter.9.cloned.1.call-start = ((), (), s32[]{:S(2)}) async-start(), calls=%async_computation.10 | async-start | bytes 9437184 | tf_op jit(solution)/shard_map/reduce_scatter | solution.py:1173
  535.4 19.1 %collective-permute-start.44 = (bf16[2,1024,256]{2,1,0:T(8,128)(2,1)}, bf16[2,1024,256]{2,1,0:T(8,128)(2,1)}, u32[]{:S(2)}, u32[]{:S(2)}) collective-permute-start(bf16[2,1024,256]{2,1,0:T(8,128)(2,1)} %get-tuple-element.183), channel_id=1, source_target_pairs={{0,8},{8,0},{16,24},{24,16},{1,9},{9,1},{17,25},{25,17},{2,10},{10... | collective-permute-start | bytes 3145736 | tf_op jit(solution)/shard_map/ppermute | solution.py:107
  535.8 20.1 %collective-permute-start.45 = (bf16[2,1024,256]{2,1,0:T(8,128)(2,1)}, bf16[2,1024,256]{2,1,0:T(8,128)(2,1)S(1)}, u32[]{:S(2)}, u32[]{:S(2)}) collective-permute-start(bf16[2,1024,256]{2,1,0:T(8,128)(2,1)} %get-tuple-element.185), channel_id=1, source_target_pairs={{0,16},{8,24},{16,0},{24,8},{1,17},{9,25},{17,1},{25,9},{2,18},{10... | collective-permute-start | bytes 3145736 | tf_op jit(solution)/shard_map/ppermute | solution.py:107
  575.1 27.1 %collective-permute-start.49 = (bf16[256,2048]{1,0:T(8,128)(2,1)}, bf16[256,2048]{1,0:T(8,128)(2,1)S(1)}, u32[]{:S(2)}, u32[]{:S(2)}) collective-permute-start(bf16[256,2048]{1,0:T(8,128)(2,1)} %reduce-scatter.5.cloned.1.call-done), channel_id=1, source_target_pairs={{0,16},{8,24},{16,0},{24,8},{1,17},{9,25},{17,1},{25,9},{2,18},{10... | collective-permute-start | bytes 3145736 | tf_op jit(solution)/shard_map/ppermute | solution.py:107
  575.1 27.2 %collective-permute-start.48 = (bf16[256,2048]{1,0:T(8,128)(2,1)}, bf16[256,2048]{1,0:T(8,128)(2,1)S(1)}, u32[]{:S(2)}, u32[]{:S(2)}) collective-permute-start(bf16[256,2048]{1,0:T(8,128)(2,1)} %reduce-scatter.5.cloned.1.call-done), channel_id=1, source_target_pairs={{0,8},{8,0},{16,24},{24,16},{1,9},{9,1},{17,25},{25,17},{2,10},{10... | collective-permute-start | bytes 3145736 | tf_op jit(solution)/shard_map/ppermute | solution.py:107
  617.2 31.9 %collective-permute-start.52 = (bf16[2,256,1024]{2,1,0:T(8,128)(2,1)S(1)}, bf16[2,256,1024]{2,1,0:T(8,128)(2,1)S(1)}, u32[]{:S(2)}, u32[]{:S(2)}) collective-permute-start(bf16[2,256,1024]{2,1,0:T(8,128)(2,1)S(1)} %copy-done.81), channel_id=1, source_target_pairs={{0,8},{8,0},{16,24},{24,16},{1,9},{9,1},{17,25},{25,17},{2,10},{10... | collective-permute-start | bytes 3145736 | tf_op jit(solution)/shard_map/ppermute | solution.py:107
  617.2 33.1 %collective-permute-start.53 = (bf16[2,256,1024]{2,1,0:T(8,128)(2,1)S(1)}, bf16[2,256,1024]{2,1,0:T(8,128)(2,1)S(1)}, u32[]{:S(2)}, u32[]{:S(2)}) collective-permute-start(bf16[2,256,1024]{2,1,0:T(8,128)(2,1)S(1)} %copy-done.80), channel_id=1, source_target_pairs={{0,16},{8,24},{16,0},{24,8},{1,17},{9,25},{17,1},{25,9},{2,18},{10... | collective-permute-start | bytes 3145736 | tf_op jit(solution)/shard_map/ppermute | solution.py:107
  619.8 23.2 %collective-permute-start.57 = (bf16[4,64,256]{2,1,0:T(8,128)(2,1)S(1)}, bf16[4,64,256]{2,1,0:T(8,128)(2,1)S(1)}, u32[]{:S(2)}, u32[]{:S(2)}) collective-permute-start(bf16[4,64,256]{2,1,0:T(8,128)(2,1)S(1)} %add_convert_fusion.14), channel_id=1, source_target_pairs={{0,6},{1,7},{2,4},{3,5},{4,2},{5,3},{6,0},{7,1},{8,14},{9,15},{10,... | collective-permute-start | bytes 393224 | tf_op jit(solution)/shard_map/ppermute | solution.py:196
  656.1 151.6 %reduce-scatter.11.cloned.1.call-start = ((), (), s32[]{:S(2)}) async-start(), calls=%async_computation.11 | async-start | bytes 5898240 | tf_op jit(solution)/shard_map/reduce_scatter | solution.py:1173
  662.6 55.0 %collective-permute-start.60 = (bf16[256,2048]{1,0:T(8,128)(2,1)}, bf16[256,2048]{1,0:T(8,128)(2,1)S(1)}, u32[]{:S(2)}, u32[]{:S(2)}) collective-permute-start(bf16[256,2048]{1,0:T(8,128)(2,1)} %reduce-scatter.7.cloned.1.call-done), channel_id=1, source_target_pairs={{0,16},{8,24},{16,0},{24,8},{1,17},{9,25},{17,1},{25,9},{2,18},{10... | collective-permute-start | bytes 3145736 | tf_op jit(solution)/shard_map/ppermute | solution.py:107
  662.8 54.8 %collective-permute-start.59 = (bf16[256,2048]{1,0:T(8,128)(2,1)}, bf16[256,2048]{1,0:T(8,128)(2,1)}, u32[]{:S(2)}, u32[]{:S(2)}) collective-permute-start(bf16[256,2048]{1,0:T(8,128)(2,1)} %reduce-scatter.7.cloned.1.call-done), channel_id=1, source_target_pairs={{0,8},{8,0},{16,24},{24,16},{1,9},{9,1},{17,25},{25,17},{2,10},{10... | collective-permute-start | bytes 3145736 | tf_op jit(solution)/shard_map/ppermute | solution.py:107
  680.8 18.0 %collective-permute-start.62 = (bf16[256,1024]{1,0:T(8,128)(2,1)S(1)}, bf16[256,1024]{1,0:T(8,128)(2,1)S(1)}, u32[]{:S(2)}, u32[]{:S(2)}) collective-permute-start(bf16[256,1024]{1,0:T(8,128)(2,1)S(1)} %copy-done.53), channel_id=1, source_target_pairs={{0,8},{8,0},{16,24},{24,16},{1,9},{9,1},{17,25},{25,17},{2,10},{10... | collective-permute-start | bytes 1572872 | tf_op jit(solution)/shard_map/ppermute | solution.py:107
  684.7 30.3 %collective-permute-start.63 = (bf16[2,256,1024]{2,1,0:T(8,128)(2,1)S(1)}, bf16[2,256,1024]{2,1,0:T(8,128)(2,1)S(1)}, u32[]{:S(2)}, u32[]{:S(2)}) collective-permute-start(bf16[2,256,1024]{2,1,0:T(8,128)(2,1)S(1)} %pad_maximum_fusion.8), channel_id=1, source_target_pairs={{0,8},{8,0},{16,24},{24,16},{1,9},{9,1},{17,25},{25,17},{2,10},{10... | collective-permute-start | bytes 3145736 | tf_op jit(solution)/shard_map/ppermute | solution.py:107
  695.7 20.0 %collective-permute-start.64 = (bf16[2,256,1024]{2,1,0:T(8,128)(2,1)S(1)}, bf16[2,256,1024]{2,1,0:T(8,128)(2,1)S(1)}, u32[]{:S(2)}, u32[]{:S(2)}) collective-permute-start(bf16[2,256,1024]{2,1,0:T(8,128)(2,1)S(1)} %slice.483), channel_id=1, source_target_pairs={{0,16},{8,24},{16,0},{24,8},{1,17},{9,25},{17,1},{25,9},{2,18},{10... | collective-permute-start | bytes 3145736 | tf_op jit(solution)/shard_map/ppermute | solution.py:107
  756.7 22.6 %collective-permute-start.70 = (bf16[256,2048]{1,0:T(8,128)(2,1)}, bf16[256,2048]{1,0:T(8,128)(2,1)}, u32[]{:S(2)}, u32[]{:S(2)}) collective-permute-start(bf16[256,2048]{1,0:T(8,128)(2,1)} %reduce-scatter.9.cloned.1.call-done), channel_id=1, source_target_pairs={{0,16},{8,24},{16,0},{24,8},{1,17},{9,25},{17,1},{25,9},{2,18},{10... | collective-permute-start | bytes 3145736 | tf_op jit(solution)/shard_map/ppermute | solution.py:107
  758.2 22.5 %collective-permute-start.69 = (bf16[256,2048]{1,0:T(8,128)(2,1)}, bf16[256,2048]{1,0:T(8,128)(2,1)}, u32[]{:S(2)}, u32[]{:S(2)}) collective-permute-start(bf16[256,2048]{1,0:T(8,128)(2,1)} %reduce-scatter.9.cloned.1.call-done), channel_id=1, source_target_pairs={{0,8},{8,0},{16,24},{24,16},{1,9},{9,1},{17,25},{25,17},{2,10},{10... | collective-permute-start | bytes 3145736 | tf_op jit(solution)/shard_map/ppermute | solution.py:107
  (128 other events, 1823.4 us)
Sparse Core Ops, SparseCore 0:
  49.1 80.7 all-gather.4
  137.4 120.9 all-gather.6
  271.9 91.9 all-gather.8
  365.4 45.8 all-gather.10
  424.2 106.9 reduce-scatter.4
  533.3 87.9 reduce-scatter.6
  655.5 89.7 reduce-scatter.8
  748.1 59.5 reduce-scatter.10
where the time goes:
time: 880 us; the launch traced here: 870 us
  waiting for transfers between devices  339 us (39%)
  Pallas kernels  174 us (20%)
  starting transfers between devices  112 us (13%)
  local copies, waits for them, and re-layouts  98.4 us (11%)
  other arithmetic  69.4 us (8%)
  matrix products  60.8 us (7%)
  between operations  16.3 us (2%)
    ppermute x66, waiting for transfers between devices, to_rep(): return lax.ppermute(block, 'rep', route)  263 us
    ppermute x66, starting transfers between devices, to_rep(): return lax.ppermute(block, 'rep', route)  75 us
    pallas_call x1, Pallas kernels, backward_products(): pl.pallas_call(backward_kernel, out_shape=[grads] * 2 + [piece] * 8, grid...  48.1 us
    dot_general x5, matrix products, weight_grad(): lax.dot_general(rows, grad_rows, (((0,), (0,)), ((), ())), preferred_elem...  45.8 us
    unnamed x198, local copies, waits for them, and re-layouts  41.5 us
    ppermute x14, waiting for transfers between devices, add_all(): others.append(lax.ppermute(low, axis, route).astype(jnp.float32))  35.2 us
    ppermute x14, starting transfers between devices, add_all(): others.append(lax.ppermute(low, axis, route).astype(jnp.float32))  32.9 us
    pallas_call x1, Pallas kernels, adam(): pl.pallas_call(functools.partial(adam_kernel, batch), out_shape=[jax.Shap...  27.7 us
  transfers between devices with their start and end apart: 92, of which 50 were waited for; matrix products, arithmetic and copies ran while one was open for 24% of the time, Pallas kernels for 16%

commit v1 on v0

--- a/solution.py
+++ b/solution.py
@@ -1191,6 +1191,10 @@
         band_number, glob_spots, wide_cosine, wide_sine, queries, grad_attended, lse, pair_blocks
     )
     down_first, *grad_blocks = after(down_first, *grad_blocks)
+    attended_all, *grad_blocks = lax.optimization_barrier((attended_all, *grad_blocks))
+    g_output = weight_grad(attended_all, grad_columns)
+    g_output = by_place(g_output.reshape(rep_total, q_width, -1)).reshape(D, -1)
+    s_output = over_tokens(g_output)
     down_second = gather_second(down_first)
     branch_pieces, *down_second = after(tuple(branch_pieces), *down_second)
     branch_first = sum_first(branch_pieces) if aligned else (own_sum(branch_pieces[0]),)
@@ -1210,8 +1214,8 @@
         glob_grads = add_all(glob_both.astype(jnp.bfloat16), "fsdp", 2)
     else:
         glob_grads = add_all(grad_blocks[-1], "fsdp")
-    branch_first, g_up, glob_grads, s_gate, *returned = lax.optimization_barrier(
-        (branch_first, g_up, glob_grads, s_gate, *returned)
+    branch_first, g_up, glob_grads, s_gate, g_output, *returned = lax.optimization_barrier(
+        (branch_first, g_up, glob_grads, s_gate, g_output, *returned)
     )
     s_up = over_tokens(g_up)
     s_down = gather_join(down_second)
@@ -1221,23 +1225,24 @@
         grad_queries, grad_blocks[-2], selector_all, glob_grads, wide_cosine, wide_sine, returned
     ).reshape(-1, q_width + 2 * kv_width)
     grad_normed_parts = mul_back(grad_inner, w_inner).astype(jnp.bfloat16).reshape(rep_total, tok_count, D)
+    gate_first, grad_normed_parts = after(gate_first, grad_normed_parts)
     if square():
         normed_first = sum_first(split_pieces(grad_normed_parts))
     else:
         normed_first = (rep_scatter(grad_normed_parts),)
     grad_inner, grad_normed_parts = lax.optimization_barrier((grad_inner, grad_normed_parts))
     g_inner = weight_grad(normed_one_all, grad_inner)
-    attended_all, g_inner = lax.optimization_barrier((attended_all, g_inner))
-    g_output = weight_grad(attended_all, grad_columns)
-    g_output = by_place(g_output.reshape(rep_total, q_width, -1)).reshape(D, -1)
-    g_attn = with_layout_constraint(jnp.concatenate([g_inner, g_output], 1), Layout((0, 1)))
+    g_attn = with_layout_constraint(g_inner, Layout((0, 1)))
     gate_first, block_out, *normed_first = after(gate_first, block_out, *normed_first)
     gate_second = gather_second(gate_first)
     grad_normed_one = sum_second(normed_first) if square() else normed_first[0]
-    gate_second, s_up, g_attn, grad_normed_one = after(gate_second, s_up, g_attn, grad_normed_one)
+    gate_second, s_up, g_attn, grad_normed_one, s_output = after(
+        gate_second, s_up, g_attn, grad_normed_one, s_output
+    )
     s_attn = over_tokens(g_attn)
     s_gate = gather_join(gate_second)
     up_first = gather_first(s_up)
+    s_output = rep_gather(s_output)
     grad_input = grad_middle + norm_back(residual, scale_one, gains[0], grad_normed_one)
 
     gain_terms = jnp.stack(
@@ -1254,7 +1259,9 @@
     up_first, sums = after(up_first, sums)
     s_up = gather_join(gather_second(up_first))
     sums = add_all(add_all(sums, "rep"), "fsdp")
-    sums, s_attn, s_up, s_gate, s_down = lax.optimization_barrier((sums, s_attn, s_up, s_gate, s_down))
+    sums, s_attn, s_up, s_gate, s_down, s_output = lax.optimization_barrier(
+        (sums, s_attn, s_up, s_gate, s_down, s_output)
+    )
     gain_grad, square_total = sums[: 2 * D].reshape(2, D), sums[2 * D :]
 
     slot_ids = jnp.arange(tile_total, dtype=jnp.int32)
@@ -1262,16 +1269,16 @@
     own_slots = place * own_count + jnp.arange(own_count, dtype=jnp.int32)
     owned_tiles = jnp.take(inverse, own_slots, mode="clip")
     if aligned:
-        sources = [rep_gather(s_attn), s_gate, s_up, s_down]
+        sources = [rep_gather(s_attn), s_output, s_gate, s_up, s_down]
         where = np.zeros((4, rep_total, tile_total), np.int32)
         first_col = 0
         for kind, grid in enumerate(layout):
             rows, cols = grid.shape[1:]
-            first_col = 0 if kind >= 4 else first_col
+            first_col = 0 if kind >= 3 else first_col
             for there in range(rep_total):
                 numbers = grid[there].reshape(-1)
                 at = np.arange(rows * cols)
-                where[0, :, numbers] = max(kind - 3, 0)
+                where[0, :, numbers] = max(kind - 2, 0)
                 where[2, :, numbers] = (at // cols * BLK)[:, None]
                 where[3, :, numbers] = (at % cols * BLK + first_col)[:, None]
                 for here in range(rep_total):
@@ -1280,9 +1287,9 @@
         tile_spots = lax.dynamic_index_in_dim(jnp.asarray(where), place, 1, False)
         meta = jnp.take(tile_spots, owned_tiles, axis=1, mode="clip")
     else:
-        splits = [0, q_width, q_width + kv_width, q_width + 2 * kv_width, s_attn.shape[1]]
+        splits = [0, q_width, q_width + kv_width, q_width + 2 * kv_width]
         stacks = [rep_gather(s_attn[:, low:high]) for low, high in zip(splits, splits[1:])]
-        stacks += [s_gate, s_up, s_down]
+        stacks += [s_output, s_gate, s_up, s_down]
         sources = [band_tiles(join_slices(stacks, band_total, rep_total))]
         meta = jnp.stack([0 * owned_tiles, owned_tiles, 0 * owned_tiles, 0 * owned_tiles], 0)
     slot_rates = jnp.take(kind_rates(band_total), owned_tiles, mode="clip")

time: 880 us -> 893 us (1.015)
    ppermute x66 -> x70, waiting for transfers between devices: 263 us -> 253 us  [to_rep(): return lax.ppermute(block, 'rep', route)]
    unnamed x198 -> x202, local copies, waits for them, and re-layouts: 41.5 us -> 46.3 us
    ppermute x66 -> x70, starting transfers between devices: 75 us -> 78.6 us  [to_rep(): return lax.ppermute(block, 'rep', route)]
  transfers between devices with their start and end apart: 92 -> 97, of which waited for: 50 -> 46; matrix products, arithmetic and copies ran while one was open for 24% -> 24% of each run, Pallas kernels for 16% -> 16%
where the time goes in v1:
time: 893 us; the launch traced here: 882 us
  waiting for transfers between devices  339 us (38%)
  Pallas kernels  174 us (19%)
  starting transfers between devices  116 us (13%)
  local copies, waits for them, and re-layouts  106 us (12%)
  other arithmetic  69.1 us (8%)
  matrix products  61.8 us (7%)
  between operations  16 us (2%)
    ppermute x70, waiting for transfers between devices, to_rep(): return lax.ppermute(block, 'rep', route)  253 us
    ppermute x70, starting transfers between devices, to_rep(): return lax.ppermute(block, 'rep', route)  78.6 us
    pallas_call x1, Pallas kernels, backward_products(): pl.pallas_call(backward_kernel, out_shape=[grads] * 2 + [piece] * 8, grid...  48.1 us
    dot_general x5, matrix products, weight_grad(): lax.dot_general(rows, grad_rows, (((0,), (0,)), ((), ())), preferred_elem...  46.9 us
    unnamed x202, local copies, waits for them, and re-layouts  46.3 us
    ppermute x14, waiting for transfers between devices, add_all(): others.append(lax.ppermute(low, axis, route).astype(jnp.float32))  43.5 us
    ppermute x14, starting transfers between devices, add_all(): others.append(lax.ppermute(low, axis, route).astype(jnp.float32))  33.7 us
    ppermute x2, waiting for transfers between devices, shifted(): return lax.ppermute(block, axis, route)  30.9 us
  transfers between devices with their start and end apart: 97, of which 46 were waited for; matrix products, arithmetic and copies ran while one was open for 24% of the time, Pallas kernels for 16%

profile of v1, /device:TPU:0, one launch (start us, length us, event | category | flops | bytes accessed | tf_op | source)
XLA Modules:
  0.0 881.9 jit_solution(7491216888408076809)
XLA Ops:
  10.4 4.0 convert.30
  23.6 12.8 %collective-permute-done.4 = bf16[2,256,640]{2,1,0:T(8,128)(2,1)S(1)} collective-permute-done((bf16[2,256,640]{2,1,0:T(8,128)(2,1)S(1)}, bf16[2,256,640]{2,1,0:T(8,128)(2,1)S(1)}, u32[]{:S(2)}, u32[]{:S(2)}) %collective-permute-start.4) | collective-permute-done | bytes 655392 | tf_op jit(solution)/shard_map/ppermute | solution.py:107
  40.6 5.7 collective-permute-done.5
  76.1 16.0 %collective-permute-done.9.refs_2_ = bf16[116,64,128]{2,1,0:T(8,128)(2,1)} collective-permute-done((bf16[116,64,128]{2,1,0:T(8,128)(2,1)S(1)}, bf16[116,64,128]{2,1,0:T(8,128)(2,1)}, u32[]{:S(2)}, u32[]{:S(2)}) %collective-permute-start.9) | collective-permute-done | bytes 1900576 | tf_op jit(solution)/shard_map/ppermute | solution.py:107
  99.5 27.9 %collective-permute-done.2 = bf16[72,2048]{1,0:T(8,128)(2,1)} collective-permute-done((bf16[72,2048]{1,0:T(8,128)(2,1)}, bf16[72,2048]{1,0:T(8,128)(2,1)}, u32[]{:S(2)}, u32[]{:S(2)}) %collective-permute-start.2) | collective-permute-done | bytes 294944 | tf_op jit(solution)/shard_map/ppermute | solution.py:196
  131.3 5.8 shard_map.241
  142.3 28.7 %collective-permute-done.12 = bf16[352,2048]{1,0:T(8,128)(2,1)S(1)} collective-permute-done((bf16[352,2048]{1,0:T(8,128)(2,1)}, bf16[352,2048]{1,0:T(8,128)(2,1)S(1)}, u32[]{:S(2)}, u32[]{:S(2)}) %collective-permute-start.12) | collective-permute-done | bytes 1441824 | tf_op jit(solution)/shard_map/ppermute | solution.py:107
  174.5 13.8 %collective-permute-done.14 = bf16[176,2048]{1,0:T(8,128)(2,1)S(1)} collective-permute-done((bf16[176,2048]{1,0:T(8,128)(2,1)S(1)}, bf16[176,2048]{1,0:T(8,128)(2,1)S(1)}, u32[]{:S(2)}, u32[]{:S(2)}) %collective-permute-start.14) | collective-permute-done | bytes 720928 | tf_op jit(solution)/shard_map/ppermute | solution.py:107
  192.6 6.1 fusion.x_ref
  198.8 4.6 shard_map.242
  205.7 21.9 %collective-permute-done.20.refs_0_ = bf16[4,256,256]{2,1,0:T(8,128)(2,1)S(1)} collective-permute-done((bf16[4,256,256]{2,1,0:T(8,128)(2,1)}, bf16[4,256,256]{2,1,0:T(8,128)(2,1)S(1)}, u32[]{:S(2)}, u32[]{:S(2)}) %collective-permute-start.20) | collective-permute-done | bytes 524320 | tf_op jit(solution)/shard_map/ppermute | solution.py:280
  248.8 17.2 %shard_map.244 = (bf16[4,256,512]{2,1,0:T(8,128)(2,1)S(1)}, f32[4,8,256]{2,1,0:T(8,128)S(1)}) custom-call(s32[1]{0:T(128)} %bitcast.25.band_ref, f32[4,64,128]{2,1,0:T(8,128)S(1)} %broadcast_in_dim.83.gpos_ref, bf16[4,256,512]{2,1,0:T(8,128)(2,1)S(1)} %copy-done.18, bf16[4,256,256]{2,1,0:T(8,128)(2,1)S(1)} %copy-done.13, ...), custom_call_target="tpu_custom_call" | custom-call | flops 6979321856 | bytes 2097152 | tf_op jit(solution)/shard_map/pallas_call | solution.py:747
  266.1 5.4 shard_map.245
  273.9 21.2 %collective-permute-done.23 = bf16[4,256,512]{2,1,0:T(8,128)(2,1)S(1)} collective-permute-done((bf16[4,256,512]{2,1,0:T(8,128)(2,1)S(1)}, bf16[4,256,512]{2,1,0:T(8,128)(2,1)S(1)}, u32[]{:S(2)}, u32[]{:S(2)}) %collective-permute-start.23) | collective-permute-done | bytes 1048608 | tf_op jit(solution)/shard_map/ppermute | solution.py:107
  298.2 9.6 %collective-permute-done.24 = bf16[2,256,512]{2,1,0:T(8,128)(2,1)S(1)} collective-permute-done((bf16[2,256,512]{2,1,0:T(8,128)(2,1)S(1)}, bf16[2,256,512]{2,1,0:T(8,128)(2,1)S(1)}, u32[]{:S(2)}, u32[]{:S(2)}) %collective-permute-start.24) | collective-permute-done | bytes 524320 | tf_op jit(solution)/shard_map/ppermute | solution.py:107
  315.9 6.1 collective-permute-done.28
  337.0 21.9 %collective-permute-done.29 = bf16[256,2048]{1,0:T(8,128)(2,1)S(1)} collective-permute-done((bf16[256,2048]{1,0:T(8,128)(2,1)S(1)}, bf16[256,2048]{1,0:T(8,128)(2,1)S(1)}, u32[]{:S(2)}, u32[]{:S(2)}) %collective-permute-start.29) | collective-permute-done | bytes 1048608 | tf_op jit(solution)/shard_map/ppermute | solution.py:107
  363.0 7.7 collective-permute-done.31
  374.3 24.5 %shard_map.246 = (bf16[1024,2048]{1,0:T(8,128)(2,1)S(1)}, bf16[1024,2048]{1,0:T(8,128)(2,1)}, bf16[1024,2048]{1,0:T(8,128)(2,1)}) custom-call(bf16[1024,2048]{1,0:T(8,128)(2,1)} %constant_dynamic-update-slice_fusion.5.x_ref, bf16[8,24,2,64,256]{4,3,2,1,0:T(8,128)(2,1)} %bitcast.289, bf16[8,16,2,64,256]{4,3,2,1,0:T(8,128)(2,1)} %bitcast.291), custom_call_target="tpu_custom_call" | custom-call | flops 536870912 | bytes 4194304 | tf_op jit(solution)/shard_map/pallas_call | solution.py:518
  406.6 6.7 collective-permute-done.35
  415.4 11.4 %convolution_convert_fusion.2 = bf16[2048,2048]{1,0:T(8,128)(2,1)} fusion(bf16[1024,2048]{1,0:T(8,128)(2,1)S(1)} %copy-done.81, bf16[1024,2048]{1,0:T(8,128)(2,1)S(1)} %constant_dynamic-update-slice_fusion.10.top_ref), kind=kOutput, calls=%fused_computation.8 | convolution fusion | flops 8594128896 | bytes 16777216 | tf_op jit(solution)/shard_map/dot_general | solution.py:1093
  427.0 48.1 %shard_map.247 = (bf16[1024,2048]{1,0:T(8,128)(2,1)}, bf16[1024,2048]{1,0:T(8,128)(2,1)}, bf16[2,256,1024]{2,1,0:T(8,128)(2,1)}, bf16[2,256,1024]{2,1,0:T(8,128)...) custom-call(bf16[1024,2048]{1,0:T(8,128)(2,1)} %copy-done.59, ...), custom_call_target="tpu_custom_call" | custom-call | flops 34359738368 | bytes 33554432 | tf_op jit(solution)/shard_map/pallas_call | solution.py:615
  477.4 14.4 %convolution_convert_fusion.1 = bf16[2048,2048]{1,0:T(8,128)(2,1)} fusion(bf16[1024,2048]{1,0:T(8,128)(2,1)} %constant_dynamic-update-slice_fusion.5.x_ref, bf16[1024,2048]{1,0:T(8,128)(2,1)} %get-tuple-element.182), kind=kOutput, calls=%fused_computation.7 | convolution fusion | flops 8594128896 | bytes 16777216 | tf_op jit(solution)/shard_map/dot_general | solution.py:1093
  491.8 4.5 collective-permute-done.37
  503.4 7.0 collective-permute-done.39
  513.2 4.1 multiply_reduce_fusion.1
  527.4 3.8 collective-permute-done.43
  534.1 3.7 shard_map.248
  540.5 13.6 %convolution_convert_fusion = bf16[2048,2048]{1,0:T(8,128)(2,1)} fusion(bf16[1024,2048]{1,0:T(8,128)(2,1)} %constant_dynamic-update-slice_fusion.5.x_ref, bf16[1024,2048]{1,0:T(8,128)(2,1)S(1)} %copy-done.82), kind=kOutput, calls=%fused_computation.6 | convolution fusion | flops 8594128896 | bytes 16777216 | tf_op jit(solution)/shard_map/dot_general | solution.py:1093
  564.7 10.6 %collective-permute-done.46 = bf16[1024,256]{1,0:T(8,128)(2,1)S(1)} collective-permute-done((bf16[1024,256]{1,0:T(8,128)(2,1)S(1)}, bf16[1024,256]{1,0:T(8,128)(2,1)S(1)}, u32[]{:S(2)}, u32[]{:S(2)}) %collective-permute-start.46) | collective-permute-done | bytes 524320 | tf_op jit(solution)/shard_map/ppermute | solution.py:107
  579.1 25.9 %shard_map.249 = (bf16[4,256,512]{2,1,0:T(8,128)(2,1)S(1)}, bf16[4,256,256]{2,1,0:T(8,128)(2,1)S(1)}, bf16[4,256,256]{2,1,0:T(8,128)(2,1)S(1)}, f32[4,256,256]{2,1,0:T(8,128)S(1)}, bf16[4,64,256]{2,1,0:T(8,128)(2,1)S(1)}) custom-call(s32[1]{0:T(128)} %bitcast.25.band_ref, f32[4,64,128]{2,1,0:T(8,128)S(1)} %broadcast_in_dim.83.gpos_ref, ...), custom_call_target="tpu_custom_call" | custom-call | flops 17448304640 | bytes 4194304 | tf_op jit(solution)/shard_map/pallas_call | solution.py:833
  612.4 9.4 %collective-permute-done.51 = bf16[128,2048]{1,0:T(8,128)(2,1)S(1)} collective-permute-done((bf16[128,2048]{1,0:T(8,128)(2,1)S(1)}, bf16[128,2048]{1,0:T(8,128)(2,1)S(1)}, u32[]{:S(2)}, u32[]{:S(2)}) %collective-permute-start.51) | collective-permute-done | bytes 524320 | tf_op jit(solution)/shard_map/ppermute | solution.py:107
  627.4 19.5 %collective-permute-start.57 = (bf16[4,64,256]{2,1,0:T(8,128)(2,1)S(1)}, bf16[4,64,256]{2,1,0:T(8,128)(2,1)S(1)}, u32[]{:S(2)}, u32[]{:S(2)}) collective-permute-start(bf16[4,64,256]{2,1,0:T(8,128)(2,1)S(1)} %add_convert_fusion.14), channel_id=1, source_target_pairs={{0,6},{1,7},{2,4},{3,5},{4,2},{5,3},{6,0},{7,1},{8,14},{9,15},{10,... | collective-permute-start | bytes 393224 | tf_op jit(solution)/shard_map/ppermute | solution.py:196
  649.9 3.6 collective-permute-done.57
  654.8 9.6 %collective-permute-done.56 = bf16[4,64,256]{2,1,0:T(8,128)(2,1)S(1)} collective-permute-done((bf16[4,64,256]{2,1,0:T(8,128)(2,1)S(1)}, bf16[4,64,256]{2,1,0:T(8,128)(2,1)S(1)}, u32[]{:S(2)}, u32[]{:S(2)}) %collective-permute-start.56) | collective-permute-done | bytes 131104 | tf_op jit(solution)/shard_map/ppermute | solution.py:196
  667.5 8.9 %collective-permute-done.58.refs_0_ = bf16[4,256,256]{2,1,0:T(8,128)(2,1)} collective-permute-done((bf16[4,256,256]{2,1,0:T(8,128)(2,1)}, bf16[4,256,256]{2,1,0:T(8,128)(2,1)}, u32[]{:S(2)}, u32[]{:S(2)}) %collective-permute-start.58) | collective-permute-done | bytes 524320 | tf_op jit(solution)/shard_map/ppermute | solution.py:280
  682.8 5.5 slice.413
  689.9 5.0 shard_map.250
  694.9 5.9 convolution_convert_fusion.3
  705.1 9.1 %collective-permute-done.61 = bf16[256,1024]{1,0:T(8,128)(2,1)} collective-permute-done((bf16[256,1024]{1,0:T(8,128)(2,1)}, bf16[256,1024]{1,0:T(8,128)(2,1)}, u32[]{:S(2)}, u32[]{:S(2)}) %collective-permute-start.61) | collective-permute-done | bytes 524320 | tf_op jit(solution)/shard_map/ppermute | solution.py:107
  717.5 15.4 %collective-permute-done.63 = bf16[2,256,1024]{2,1,0:T(8,128)(2,1)S(1)} collective-permute-done((bf16[2,256,1024]{2,1,0:T(8,128)(2,1)S(1)}, bf16[2,256,1024]{2,1,0:T(8,128)(2,1)S(1)}, u32[]{:S(2)}, u32[]{:S(2)}) %collective-permute-start.63) | collective-permute-done | bytes 1048608 | tf_op jit(solution)/shard_map/ppermute | solution.py:107
  736.9 5.1 convolution_convert_fusion.4
  750.3 5.8 collective-permute-done.66
  756.1 11.2 %reduce-scatter.10.cloned.1.call-done = bf16[256,2048]{1,0:T(8,128)(2,1)} async-done(((bf16[2048,2048]{1,0:T(8,128)(2,1)}), bf16[256,2048]{1,0:T(8,128)(2,1)}) %reduce-scatter.10.cloned.1.call-update) | async-done | bytes 1048592 | tf_op jit(solution)/shard_map/reduce_scatter | solution.py:1173
  801.3 3.9 collective-permute-done.82
  832.6 7.0 collective-permute-done.85
  841.4 4.6 collective-permute-done.86
  847.2 27.8 %shard_map.251 = (f32[116,128,128]{2,1,0:T(8,128)}, f32[116,128,128]{2,1,0:T(8,128)}, f32[116,128,128]{2,1,0:T(8,128)}, bf16[116,128,128]{2,1,0:T(8,128)(2,1)}) custom-call(s32[4,116]{1,0:T(4,128)} %bitcast.342, f32[116]{0:T(128)} %gather_fusion.5, f32[116,128,128]{2,1,0:T(8,128)} %bitcast.288, f32[116,128,128]{2,1,0:T(8,128)} %bitcast.297, ...), custom_call_target="tpu_custom_call" | custom-call | flops 1946157056 | bytes 68419584 | tf_op jit(solution)/shard_map/pallas_call | solution.py:962
  (541 shorter events, 293.9 us)
Async XLA Ops:
  7.2 130.0 %all-gather.5.cloned.1.call-start = ((), (), s32[]{:S(2)}) async-start(), calls=%async_computation.5 | async-start | bytes 5898240 | tf_op jit(solution)/shard_map/all_gather | solution.py:1032
  48.7 217.4 %all-gather.7.cloned.1.call-start = ((), (), s32[]{:S(2)}) async-start(), calls=%async_computation.6 | async-start | bytes 14155776 | tf_op jit(solution)/shard_map/all_gather | solution.py:1032
  51.5 40.7 %collective-permute-start.9 = (bf16[116,64,128]{2,1,0:T(8,128)(2,1)S(1)}, bf16[116,64,128]{2,1,0:T(8,128)(2,1)}, u32[]{:S(2)}, u32[]{:S(2)}) collective-permute-start(bf16[116,64,128]{2,1,0:T(8,128)(2,1)S(1)} %get-tuple-element.144.low.refs_0_), channel_id=1, source_target_pairs={{0,16},{8,24},{16,0},{24,8},{1,17},{9,25},{17,1},{25,9},{2,18},{10... | collective-permute-start | bytes 5701640 | tf_op jit(solution)/shard_map/ppermute | solution.py:107
  52.1 44.2 %collective-permute-start.8 = (bf16[116,64,128]{2,1,0:T(8,128)(2,1)S(1)}, bf16[116,64,128]{2,1,0:T(8,128)(2,1)}, u32[]{:S(2)}, u32[]{:S(2)}) collective-permute-start(bf16[116,64,128]{2,1,0:T(8,128)(2,1)S(1)} %get-tuple-element.144.low.refs_0_), channel_id=1, source_target_pairs={{0,8},{8,0},{16,24},{24,16},{1,9},{9,1},{17,25},{25,17},{2,10},{10... | collective-permute-start | bytes 5701640 | tf_op jit(solution)/shard_map/ppermute | solution.py:107
  71.7 27.8 %collective-permute-start.3 = (bf16[72,2048]{1,0:T(8,128)(2,1)}, bf16[72,2048]{1,0:T(8,128)(2,1)}, u32[]{:S(2)}, u32[]{:S(2)}) collective-permute-start(bf16[72,2048]{1,0:T(8,128)(2,1)} %fusion.36), channel_id=1, source_target_pairs={{0,6},{1,7},{2,4},{3,5},{4,2},{5,3},{6,0},{7,1},{8,14},{9,15},{10,... | collective-permute-start | bytes 884744 | tf_op jit(solution)/shard_map/ppermute | solution.py:196
  75.0 52.5 %collective-permute-start.2 = (bf16[72,2048]{1,0:T(8,128)(2,1)}, bf16[72,2048]{1,0:T(8,128)(2,1)}, u32[]{:S(2)}, u32[]{:S(2)}) collective-permute-start(bf16[72,2048]{1,0:T(8,128)(2,1)} %fusion.36), channel_id=1, source_target_pairs={{0,4},{1,5},{2,6},{3,7},{4,0},{5,1},{6,2},{7,3},{8,12},{9,13},{10,... | collective-permute-start | bytes 884744 | tf_op jit(solution)/shard_map/ppermute | solution.py:196
  75.0 52.5 %collective-permute-start.1 = (bf16[72,2048]{1,0:T(8,128)(2,1)}, bf16[72,2048]{1,0:T(8,128)(2,1)}, u32[]{:S(2)}, u32[]{:S(2)}) collective-permute-start(bf16[72,2048]{1,0:T(8,128)(2,1)} %fusion.36), channel_id=1, source_target_pairs={{0,2},{1,3},{2,0},{3,1},{4,6},{5,7},{6,4},{7,5},{8,10},{9,11},{10,... | collective-permute-start | bytes 884744 | tf_op jit(solution)/shard_map/ppermute | solution.py:196
  94.3 36.9 %collective-permute-start.11 = (bf16[58,64,128]{2,1,0:T(8,128)(2,1)}, bf16[58,64,128]{2,1,0:T(8,128)(2,1)S(1)}, u32[]{:S(2)}, u32[]{:S(2)}) collective-permute-start(bf16[58,64,128]{2,1,0:T(8,128)(2,1)} %slice.448), channel_id=1, source_target_pairs={{0,8},{8,0},{16,24},{24,16},{1,9},{9,1},{17,25},{25,17},{2,10},{10... | collective-permute-start | bytes 2850824 | tf_op jit(solution)/shard_map/ppermute | solution.py:107
  98.5 32.8 %collective-permute-start.10 = (bf16[58,64,128]{2,1,0:T(8,128)(2,1)}, bf16[58,64,128]{2,1,0:T(8,128)(2,1)}, u32[]{:S(2)}, u32[]{:S(2)}) collective-permute-start(bf16[58,64,128]{2,1,0:T(8,128)(2,1)} %slice.447), channel_id=1, source_target_pairs={{0,16},{8,24},{16,0},{24,8},{1,17},{9,25},{17,1},{25,9},{2,18},{10... | collective-permute-start | bytes 2850824 | tf_op jit(solution)/shard_map/ppermute | solution.py:107
  137.2 237.2 %all-gather.9.cloned.1.call-start = ((), (), s32[]{:S(2)}) async-start(), calls=%async_computation.7 | async-start | bytes 9437184 | tf_op jit(solution)/shard_map/all_gather | solution.py:1032
  137.2 33.7 %collective-permute-start.12 = (bf16[352,2048]{1,0:T(8,128)(2,1)}, bf16[352,2048]{1,0:T(8,128)(2,1)S(1)}, u32[]{:S(2)}, u32[]{:S(2)}) collective-permute-start(bf16[352,2048]{1,0:T(8,128)(2,1)} %fusion.28), channel_id=1, source_target_pairs={{0,8},{8,0},{16,24},{24,16},{1,9},{9,1},{17,25},{25,17},{2,10},{10... | collective-permute-start | bytes 4325384 | tf_op jit(solution)/shard_map/ppermute | solution.py:107
  138.7 34.0 %collective-permute-start.13 = (bf16[352,2048]{1,0:T(8,128)(2,1)}, bf16[352,2048]{1,0:T(8,128)(2,1)S(1)}, u32[]{:S(2)}, u32[]{:S(2)}) collective-permute-start(bf16[352,2048]{1,0:T(8,128)(2,1)} %fusion.28), channel_id=1, source_target_pairs={{0,16},{8,24},{16,0},{24,8},{1,17},{9,25},{17,1},{25,9},{2,18},{10... | collective-permute-start | bytes 4325384 | tf_op jit(solution)/shard_map/ppermute | solution.py:107
  190.1 41.7 %collective-permute-start.17 = (bf16[116,64,128]{2,1,0:T(8,128)(2,1)S(1)}, bf16[116,64,128]{2,1,0:T(8,128)(2,1)}, u32[]{:S(2)}, u32[]{:S(2)}) collective-permute-start(bf16[116,64,128]{2,1,0:T(8,128)(2,1)S(1)} %copy-done.1), channel_id=1, source_target_pairs={{0,16},{8,24},{16,0},{24,8},{1,17},{9,25},{17,1},{25,9},{2,18},{10... | collective-permute-start | bytes 5701640 | tf_op jit(solution)/shard_map/ppermute | solution.py:107
  191.0 44.5 %collective-permute-start.16 = (bf16[116,64,128]{2,1,0:T(8,128)(2,1)S(1)}, bf16[116,64,128]{2,1,0:T(8,128)(2,1)}, u32[]{:S(2)}, u32[]{:S(2)}) collective-permute-start(bf16[116,64,128]{2,1,0:T(8,128)(2,1)S(1)} %copy-done.1), channel_id=1, source_target_pairs={{0,8},{8,0},{16,24},{24,16},{1,9},{9,1},{17,25},{25,17},{2,10},{10... | collective-permute-start | bytes 5701640 | tf_op jit(solution)/shard_map/ppermute | solution.py:107
  203.4 24.3 %collective-permute-start.20 = (bf16[4,256,256]{2,1,0:T(8,128)(2,1)}, bf16[4,256,256]{2,1,0:T(8,128)(2,1)S(1)}, u32[]{:S(2)}, u32[]{:S(2)}) collective-permute-start(bf16[4,256,256]{2,1,0:T(8,128)(2,1)} %get-tuple-element.151.refs_2_), channel_id=1, source_target_pairs={{0,2},{1,3},{2,4},{3,5},{4,6},{5,7},{8,10},{9,11},{10,12},{11,13},... | collective-permute-start | bytes 1572872 | tf_op jit(solution)/shard_map/ppermute | solution.py:280
  234.0 32.0 %collective-permute-start.19 = (bf16[58,64,128]{2,1,0:T(8,128)(2,1)}, bf16[58,64,128]{2,1,0:T(8,128)(2,1)}, u32[]{:S(2)}, u32[]{:S(2)}) collective-permute-start(bf16[58,64,128]{2,1,0:T(8,128)(2,1)} %slice.452), channel_id=1, source_target_pairs={{0,8},{8,0},{16,24},{24,16},{1,9},{9,1},{17,25},{25,17},{2,10},{10... | collective-permute-start | bytes 2850824 | tf_op jit(solution)/shard_map/ppermute | solution.py:107
  237.7 28.4 %collective-permute-start.18 = (bf16[58,64,128]{2,1,0:T(8,128)(2,1)}, bf16[58,64,128]{2,1,0:T(8,128)(2,1)}, u32[]{:S(2)}, u32[]{:S(2)}) collective-permute-start(bf16[58,64,128]{2,1,0:T(8,128)(2,1)} %slice.451), channel_id=1, source_target_pairs={{0,16},{8,24},{16,0},{24,8},{1,17},{9,25},{17,1},{25,9},{2,18},{10... | collective-permute-start | bytes 2850824 | tf_op jit(solution)/shard_map/ppermute | solution.py:107
  271.5 155.5 %all-gather.11.cloned.1.call-start = ((), (), s32[]{:S(2)}) async-start(), calls=%async_computation.8 | async-start | bytes 4718592 | tf_op jit(solution)/shard_map/all_gather | solution.py:1032
  271.5 23.6 %collective-permute-start.23 = (bf16[4,256,512]{2,1,0:T(8,128)(2,1)S(1)}, bf16[4,256,512]{2,1,0:T(8,128)(2,1)S(1)}, u32[]{:S(2)}, u32[]{:S(2)}) collective-permute-start(bf16[4,256,512]{2,1,0:T(8,128)(2,1)S(1)} %get-tuple-element.154), channel_id=1, source_target_pairs={{0,16},{8,24},{16,0},{24,8},{1,17},{9,25},{17,1},{25,9},{2,18},{10... | collective-permute-start | bytes 3145736 | tf_op jit(solution)/shard_map/ppermute | solution.py:107
  273.2 24.4 %collective-permute-start.22 = (bf16[4,256,512]{2,1,0:T(8,128)(2,1)S(1)}, bf16[4,256,512]{2,1,0:T(8,128)(2,1)S(1)}, u32[]{:S(2)}, u32[]{:S(2)}) collective-permute-start(bf16[4,256,512]{2,1,0:T(8,128)(2,1)S(1)} %get-tuple-element.154), channel_id=1, source_target_pairs={{0,8},{8,0},{16,24},{24,16},{1,9},{9,1},{17,25},{25,17},{2,10},{10... | collective-permute-start | bytes 3145736 | tf_op jit(solution)/shard_map/ppermute | solution.py:107
  315.4 261.3 %reduce-scatter.6.cloned.1.call-start = ((), (), s32[]{:S(2)}) async-start(), calls=%async_computation.9 | async-start | bytes 9437184 | tf_op jit(solution)/shard_map/reduce_scatter | solution.py:1173
  335.3 23.6 %collective-permute-start.29 = (bf16[256,2048]{1,0:T(8,128)(2,1)S(1)}, bf16[256,2048]{1,0:T(8,128)(2,1)S(1)}, u32[]{:S(2)}, u32[]{:S(2)}) collective-permute-start(bf16[256,2048]{1,0:T(8,128)(2,1)S(1)} %get-tuple-element.290), channel_id=1, source_target_pairs={{0,8},{8,0},{16,24},{24,16},{1,9},{9,1},{17,25},{25,17},{2,10},{10... | collective-permute-start | bytes 3145736 | tf_op jit(solution)/shard_map/ppermute | solution.py:107
  336.0 23.6 %collective-permute-start.30 = (bf16[256,2048]{1,0:T(8,128)(2,1)S(1)}, bf16[256,2048]{1,0:T(8,128)(2,1)S(1)}, u32[]{:S(2)}, u32[]{:S(2)}) collective-permute-start(bf16[256,2048]{1,0:T(8,128)(2,1)S(1)} %get-tuple-element.290), channel_id=1, source_target_pairs={{0,16},{8,24},{16,0},{24,8},{1,17},{9,25},{17,1},{25,9},{2,18},{10... | collective-permute-start | bytes 3145736 | tf_op jit(solution)/shard_map/ppermute | solution.py:107
  372.4 26.5 %collective-permute-start.34 = (bf16[256,2048]{1,0:T(8,128)(2,1)S(1)}, bf16[256,2048]{1,0:T(8,128)(2,1)}, u32[]{:S(2)}, u32[]{:S(2)}) collective-permute-start(bf16[256,2048]{1,0:T(8,128)(2,1)S(1)} %bitcast.312), channel_id=1, source_target_pairs={{0,16},{8,24},{16,0},{24,8},{1,17},{9,25},{17,1},{25,9},{2,18},{10... | collective-permute-start | bytes 3145736 | tf_op jit(solution)/shard_map/ppermute | solution.py:107
  373.3 25.6 %collective-permute-start.33 = (bf16[256,2048]{1,0:T(8,128)(2,1)S(1)}, bf16[256,2048]{1,0:T(8,128)(2,1)}, u32[]{:S(2)}, u32[]{:S(2)}) collective-permute-start(bf16[256,2048]{1,0:T(8,128)(2,1)S(1)} %bitcast.313), channel_id=1, source_target_pairs={{0,8},{8,0},{16,24},{24,16},{1,9},{9,1},{17,25},{25,17},{2,10},{10... | collective-permute-start | bytes 3145736 | tf_op jit(solution)/shard_map/ppermute | solution.py:107
  426.8 240.7 %reduce-scatter.8.cloned.1.call-start = ((), (), s32[]{:S(2)}) async-start(), calls=%async_computation.10 | async-start | bytes 9437184 | tf_op jit(solution)/shard_map/reduce_scatter | solution.py:1173
  475.1 21.2 %collective-permute-start.37 = (bf16[2,256,1024]{2,1,0:T(8,128)(2,1)}, bf16[2,256,1024]{2,1,0:T(8,128)(2,1)S(1)}, u32[]{:S(2)}, u32[]{:S(2)}) collective-permute-start(bf16[2,256,1024]{2,1,0:T(8,128)(2,1)} %get-tuple-element.179), channel_id=1, source_target_pairs={{0,8},{8,0},{16,24},{24,16},{1,9},{9,1},{17,25},{25,17},{2,10},{10... | collective-permute-start | bytes 3145736 | tf_op jit(solution)/shard_map/ppermute | solution.py:107
  475.7 23.5 %collective-permute-start.38 = (bf16[2,256,1024]{2,1,0:T(8,128)(2,1)}, bf16[2,256,1024]{2,1,0:T(8,128)(2,1)}, u32[]{:S(2)}, u32[]{:S(2)}) collective-permute-start(bf16[2,256,1024]{2,1,0:T(8,128)(2,1)} %get-tuple-element.181), channel_id=1, source_target_pairs={{0,16},{8,24},{16,0},{24,8},{1,17},{9,25},{17,1},{25,9},{2,18},{10... | collective-permute-start | bytes 3145736 | tf_op jit(solution)/shard_map/ppermute | solution.py:107
  513.1 237.2 %reduce-scatter.12.cloned.1.call-start = ((), (), s32[]{:S(2)}) async-start(), calls=%async_computation.12 | async-start | bytes 2359296 | tf_op jit(solution)/shard_map/reduce_scatter | solution.py:1173
  538.8 18.5 %collective-permute-start.44 = (bf16[2,1024,256]{2,1,0:T(8,128)(2,1)}, bf16[2,1024,256]{2,1,0:T(8,128)(2,1)}, u32[]{:S(2)}, u32[]{:S(2)}) collective-permute-start(bf16[2,1024,256]{2,1,0:T(8,128)(2,1)} %get-tuple-element.192), channel_id=1, source_target_pairs={{0,8},{8,0},{16,24},{24,16},{1,9},{9,1},{17,25},{25,17},{2,10},{10... | collective-permute-start | bytes 3145736 | tf_op jit(solution)/shard_map/ppermute | solution.py:107
  539.9 20.0 %collective-permute-start.45 = (bf16[2,1024,256]{2,1,0:T(8,128)(2,1)}, bf16[2,1024,256]{2,1,0:T(8,128)(2,1)S(1)}, u32[]{:S(2)}, u32[]{:S(2)}) collective-permute-start(bf16[2,1024,256]{2,1,0:T(8,128)(2,1)} %get-tuple-element.194), channel_id=1, source_target_pairs={{0,16},{8,24},{16,0},{24,8},{1,17},{9,25},{17,1},{25,9},{2,18},{10... | collective-permute-start | bytes 3145736 | tf_op jit(solution)/shard_map/ppermute | solution.py:107
  576.7 28.4 %collective-permute-start.49 = (bf16[256,2048]{1,0:T(8,128)(2,1)}, bf16[256,2048]{1,0:T(8,128)(2,1)S(1)}, u32[]{:S(2)}, u32[]{:S(2)}) collective-permute-start(bf16[256,2048]{1,0:T(8,128)(2,1)} %reduce-scatter.6.cloned.1.call-done), channel_id=1, source_target_pairs={{0,16},{8,24},{16,0},{24,8},{1,17},{9,25},{17,1},{25,9},{2,18},{10... | collective-permute-start | bytes 3145736 | tf_op jit(solution)/shard_map/ppermute | solution.py:107
  578.8 26.3 %collective-permute-start.48 = (bf16[256,2048]{1,0:T(8,128)(2,1)}, bf16[256,2048]{1,0:T(8,128)(2,1)S(1)}, u32[]{:S(2)}, u32[]{:S(2)}) collective-permute-start(bf16[256,2048]{1,0:T(8,128)(2,1)} %reduce-scatter.6.cloned.1.call-done), channel_id=1, source_target_pairs={{0,8},{8,0},{16,24},{24,16},{1,9},{9,1},{17,25},{25,17},{2,10},{10... | collective-permute-start | bytes 3145736 | tf_op jit(solution)/shard_map/ppermute | solution.py:107
  609.4 157.9 %reduce-scatter.10.cloned.1.call-start = ((), (), s32[]{:S(2)}) async-start(), calls=%async_computation.11 | async-start | bytes 9437184 | tf_op jit(solution)/shard_map/reduce_scatter | solution.py:1173
  624.7 40.5 %collective-permute-start.52 = (bf16[2,256,1024]{2,1,0:T(8,128)(2,1)}, bf16[2,256,1024]{2,1,0:T(8,128)(2,1)S(1)}, u32[]{:S(2)}, u32[]{:S(2)}) collective-permute-start(bf16[2,256,1024]{2,1,0:T(8,128)(2,1)} %get-tuple-element.212), channel_id=1, source_target_pairs={{0,8},{8,0},{16,24},{24,16},{1,9},{9,1},{17,25},{25,17},{2,10},{10... | collective-permute-start | bytes 3145736 | tf_op jit(solution)/shard_map/ppermute | solution.py:107
  624.9 41.4 %collective-permute-start.53 = (bf16[2,256,1024]{2,1,0:T(8,128)(2,1)}, bf16[2,256,1024]{2,1,0:T(8,128)(2,1)S(1)}, u32[]{:S(2)}, u32[]{:S(2)}) collective-permute-start(bf16[2,256,1024]{2,1,0:T(8,128)(2,1)} %get-tuple-element.214), channel_id=1, source_target_pairs={{0,16},{8,24},{16,0},{24,8},{1,17},{9,25},{17,1},{25,9},{2,18},{10... | collective-permute-start | bytes 3145736 | tf_op jit(solution)/shard_map/ppermute | solution.py:107
  627.4 26.1 %collective-permute-start.57 = (bf16[4,64,256]{2,1,0:T(8,128)(2,1)S(1)}, bf16[4,64,256]{2,1,0:T(8,128)(2,1)S(1)}, u32[]{:S(2)}, u32[]{:S(2)}) collective-permute-start(bf16[4,64,256]{2,1,0:T(8,128)(2,1)S(1)} %add_convert_fusion.14), channel_id=1, source_target_pairs={{0,6},{1,7},{2,4},{3,5},{4,2},{5,3},{6,0},{7,1},{8,14},{9,15},{10,... | collective-permute-start | bytes 393224 | tf_op jit(solution)/shard_map/ppermute | solution.py:196
  653.5 22.9 %collective-permute-start.58 = (bf16[4,256,256]{2,1,0:T(8,128)(2,1)}, bf16[4,256,256]{2,1,0:T(8,128)(2,1)}, u32[]{:S(2)}, u32[]{:S(2)}) collective-permute-start(bf16[4,256,256]{2,1,0:T(8,128)(2,1)} %get-tuple-element.348), channel_id=1, source_target_pairs={{2,0},{3,1},{4,2},{5,3},{6,4},{7,5},{10,8},{11,9},{12,10},{13,11},... | collective-permute-start | bytes 1572872 | tf_op jit(solution)/shard_map/ppermute | solution.py:280
  676.5 152.1 %reduce-scatter.14.cloned.1.call-start = ((), (), s32[]{:S(2)}) async-start(), calls=%async_computation.13 | async-start | bytes 3538944 | tf_op jit(solution)/shard_map/reduce_scatter | solution.py:1173
  676.5 26.5 %collective-permute-start.60 = (bf16[256,2048]{1,0:T(8,128)(2,1)}, bf16[256,2048]{1,0:T(8,128)(2,1)}, u32[]{:S(2)}, u32[]{:S(2)}) collective-permute-start(bf16[256,2048]{1,0:T(8,128)(2,1)} %reduce-scatter.8.cloned.1.call-done), channel_id=1, source_target_pairs={{0,16},{8,24},{16,0},{24,8},{1,17},{9,25},{17,1},{25,9},{2,18},{10... | collective-permute-start | bytes 3145736 | tf_op jit(solution)/shard_map/ppermute | solution.py:107
  677.5 25.5 %collective-permute-start.59 = (bf16[256,2048]{1,0:T(8,128)(2,1)}, bf16[256,2048]{1,0:T(8,128)(2,1)}, u32[]{:S(2)}, u32[]{:S(2)}) collective-permute-start(bf16[256,2048]{1,0:T(8,128)(2,1)} %reduce-scatter.8.cloned.1.call-done), channel_id=1, source_target_pairs={{0,8},{8,0},{16,24},{24,16},{1,9},{9,1},{17,25},{25,17},{2,10},{10... | collective-permute-start | bytes 3145736 | tf_op jit(solution)/shard_map/ppermute | solution.py:107
  689.0 25.2 %collective-permute-start.61 = (bf16[256,1024]{1,0:T(8,128)(2,1)}, bf16[256,1024]{1,0:T(8,128)(2,1)}, u32[]{:S(2)}, u32[]{:S(2)}) collective-permute-start(bf16[256,1024]{1,0:T(8,128)(2,1)} %get-tuple-element.235), channel_id=1, source_target_pairs={{0,16},{8,24},{16,0},{24,8},{1,17},{9,25},{17,1},{25,9},{2,18},{10... | collective-permute-start | bytes 1572872 | tf_op jit(solution)/shard_map/ppermute | solution.py:107
  703.3 29.6 %collective-permute-start.63 = (bf16[2,256,1024]{2,1,0:T(8,128)(2,1)S(1)}, bf16[2,256,1024]{2,1,0:T(8,128)(2,1)S(1)}, u32[]{:S(2)}, u32[]{:S(2)}) collective-permute-start(bf16[2,256,1024]{2,1,0:T(8,128)(2,1)S(1)} %pad_maximum_fusion.7), channel_id=1, source_target_pairs={{0,8},{8,0},{16,24},{24,16},{1,9},{9,1},{17,25},{25,17},{2,10},{10... | collective-permute-start | bytes 3145736 | tf_op jit(solution)/shard_map/ppermute | solution.py:107
  704.0 28.9 %collective-permute-start.64 = (bf16[2,256,1024]{2,1,0:T(8,128)(2,1)S(1)}, bf16[2,256,1024]{2,1,0:T(8,128)(2,1)S(1)}, u32[]{:S(2)}, u32[]{:S(2)}) collective-permute-start(bf16[2,256,1024]{2,1,0:T(8,128)(2,1)S(1)} %slice.407), channel_id=1, source_target_pairs={{0,16},{8,24},{16,0},{24,8},{1,17},{9,25},{17,1},{25,9},{2,18},{10... | collective-permute-start | bytes 3145736 | tf_op jit(solution)/shard_map/ppermute | solution.py:107
  773.9 21.1 %collective-permute-start.81 = (bf16[256,512]{1,0:T(8,128)(2,1)}, bf16[256,512]{1,0:T(8,128)(2,1)S(1)}, u32[]{:S(2)}, u32[]{:S(2)}) collective-permute-start(bf16[256,512]{1,0:T(8,128)(2,1)} %reduce-scatter.12.cloned.1.call-done), channel_id=1, source_target_pairs={{0,16},{8,24},{16,0},{24,8},{1,17},{9,25},{17,1},{25,9},{2,18},{10... | collective-permute-start | bytes 786440 | tf_op jit(solution)/shard_map/ppermute | solution.py:107
  775.4 21.1 %collective-permute-start.80 = (bf16[256,512]{1,0:T(8,128)(2,1)}, bf16[256,512]{1,0:T(8,128)(2,1)}, u32[]{:S(2)}, u32[]{:S(2)}) collective-permute-start(bf16[256,512]{1,0:T(8,128)(2,1)} %reduce-scatter.12.cloned.1.call-done), channel_id=1, source_target_pairs={{0,8},{8,0},{16,24},{24,16},{1,9},{9,1},{17,25},{25,17},{2,10},{10... | collective-permute-start | bytes 786440 | tf_op jit(solution)/shard_map/ppermute | solution.py:107
  776.8 30.2 %collective-permute-start.70 = (bf16[256,2048]{1,0:T(8,128)(2,1)}, bf16[256,2048]{1,0:T(8,128)(2,1)S(1)}, u32[]{:S(2)}, u32[]{:S(2)}) collective-permute-start(bf16[256,2048]{1,0:T(8,128)(2,1)} %reduce-scatter.10.cloned.1.call-done), channel_id=1, source_target_pairs={{0,16},{8,24},{16,0},{24,8},{1,17},{9,25},{17,1},{25,9},{2,18},{10... | collective-permute-start | bytes 3145736 | tf_op jit(solution)/shard_map/ppermute | solution.py:107
  777.3 29.7 %collective-permute-start.69 = (bf16[256,2048]{1,0:T(8,128)(2,1)}, bf16[256,2048]{1,0:T(8,128)(2,1)}, u32[]{:S(2)}, u32[]{:S(2)}) collective-permute-start(bf16[256,2048]{1,0:T(8,128)(2,1)} %reduce-scatter.10.cloned.1.call-done), channel_id=1, source_target_pairs={{0,8},{8,0},{16,24},{24,16},{1,9},{9,1},{17,25},{25,17},{2,10},{10... | collective-permute-start | bytes 3145736 | tf_op jit(solution)/shard_map/ppermute | solution.py:107
  (133 other events, 1552.5 us)
Sparse Core Ops, SparseCore 0:
  48.8 80.9 all-gather.4
  137.3 121.0 all-gather.6
  271.6 92.5 all-gather.8
  365.7 45.6 all-gather.10
  426.9 107.0 reduce-scatter.5
  536.1 87.9 reduce-scatter.7
  627.0 46.5 reduce-scatter.11
  676.6 90.6 reduce-scatter.9
  770.2 38.7 reduce-scatter.13
